TPU v7x, 128 devices: a whole 4x4x4 slice. The times are simulated.
128 devices in a mesh: rows: 32 (over x, z, core), sub: 4 (over y).
Axes of the slice: x: 4, y: 4, z: 4, core: 2. Of those that a mesh axis runs over, the one named last changes fastest.
Arguments:
- vectors: bfloat16 [32768, 1024], P(('rows', 'sub')), may hold values from -6 to 6
- coarse_list: int32 [32768], P(('rows', 'sub')), may hold values from 0 to 524287, as said below
- list_slot: int32 [524288], replicated, may hold values from 0 to 524287, as said below
- codes: int32 [32768, 64], P(('rows', 'sub')), may hold values from 0 to 255
- centroids: bfloat16 [524288, 1024], P(('rows', 'sub')), may hold values from -3 to 3
- rotation: bfloat16 [1024, 1024], replicated, may hold values from -0.1875 to 0.1875
- codebook: bfloat16 [64, 256, 16], replicated, may hold values from -6 to 6
Outputs:
- new_codebook: float32 [64, 256, 16], P('sub', 'rows')
- procrustes: float32 [1024, 1024], P(('rows', 'sub'))
Inputs may be any that keep to these rules, and one draw needn't show every extreme that they name: `list_slot`: a permutation. `coarse_list`: for slot s, the owning device is s // 4096 along rows+sub. Of the vectors of one device, at most 10 have lists owned by one device, and one device owns the lists of exactly 10 vectors of every device.
All inputs are finite; a program needn't handle non-finite values.
Results may differ from a plain program's by a relative error of at most 0.0042.
Values may be sent and summed in bfloat16 or wider, within the bound.
A program may use at most 128 MiB of HBM per device.

v0:
```python
import math

import jax
import jax.numpy as jnp
from jax import lax
from jax.sharding import PartitionSpec as P

D = 1024
M = 64


def reconstruct(row_codes, codebook):
    row_count, subspaces = row_codes.shape
    block_rows = math.gcd(row_count, 256)
    grouped = row_codes.reshape(row_count // block_rows, block_rows, subspaces)
    levels = jnp.arange(codebook.shape[1], dtype=jnp.int32)

    def decode_block(labels):
        onehot = (labels[:, :, None] == levels).astype(jnp.bfloat16)
        rebuilt = jnp.einsum("bmk,mkd->bmd", onehot, codebook, preferred_element_type=jnp.float32)
        return rebuilt.astype(jnp.bfloat16).reshape(block_rows, -1)

    return lax.map(decode_block, grouped).reshape(row_count, -1)


def subspace_sums(rotated, row_codes, level_count):
    row_count, full_width = rotated.shape
    subspaces = row_codes.shape[1]
    sub_width = full_width // subspaces
    block_rows = math.gcd(row_count, 512)
    values = rotated.reshape(row_count // block_rows, block_rows, subspaces, sub_width)
    grouped = row_codes.reshape(row_count // block_rows, block_rows, subspaces)
    levels = jnp.arange(level_count, dtype=jnp.int32)

    def accumulate(running, batch_item):
        segment, labels = batch_item
        onehot = (labels[:, :, None] == levels).astype(jnp.bfloat16)
        code_total = running[0] + jnp.einsum(
            "bmk,bmd->mkd", onehot, segment, preferred_element_type=jnp.float32
        )
        counts = running[1] + jnp.sum(onehot.astype(jnp.float32), axis=0)
        return ((code_total, counts), None)

    start_state = (
        jnp.zeros((subspaces, level_count, sub_width), jnp.float32),
        jnp.zeros((subspaces, level_count), jnp.float32),
    )
    result, unused = lax.scan(accumulate, start_state, (values, grouped))
    return result


def per_device(vectors, coarse_list, list_slot, codes, centroids, rotation, codebook):
    devices = lax.axis_size(("rows", "sub"))
    tok_rows = vectors.shape[0]
    list_rows = centroids.shape[0]
    capacity = 5 * tok_rows // devices
    slot_of = list_slot[coarse_list]
    owner_of = slot_of // list_rows
    local_row = slot_of % list_rows
    owners = (owner_of[:, None] == jnp.arange(devices, dtype=jnp.int32)[None, :]).astype(jnp.int32)
    rank_of = jnp.sum((jnp.cumsum(owners, axis=0) - 1) * owners, axis=1)
    position = owner_of * capacity + rank_of
    send_vectors = jnp.zeros((devices * capacity, D), jnp.bfloat16).at[position].set(vectors)
    send_codes = jnp.full((devices * capacity, M), -1, jnp.int32).at[position].set(codes)
    send_rows = jnp.full((devices * capacity,), -1, jnp.int32).at[position].set(local_row)
    got_vectors, got_codes, got_rows = (
        lax.all_to_all(
            send_vectors.reshape(devices, capacity, D),
            ("rows", "sub"),
            split_axis=0,
            concat_axis=0,
            tiled=True,
        ),
        lax.all_to_all(
            send_codes.reshape(devices, capacity, M),
            ("rows", "sub"),
            split_axis=0,
            concat_axis=0,
            tiled=True,
        ),
        lax.all_to_all(
            send_rows.reshape(devices, capacity),
            ("rows", "sub"),
            split_axis=0,
            concat_axis=0,
            tiled=True,
        ),
    )
    got_vectors = got_vectors.reshape(devices * capacity, D)
    row_codes = got_codes.reshape(devices * capacity, M)
    got_rows = got_rows.reshape(devices * capacity)
    fetched = centroids[jnp.maximum(got_rows, 0)]
    difference = got_vectors.astype(jnp.float32) - fetched.astype(jnp.float32)
    residual = jnp.where((got_rows >= 0)[:, None], difference, 0.0).astype(jnp.bfloat16)
    rotated = jnp.dot(residual, rotation, preferred_element_type=jnp.float32).astype(jnp.bfloat16)
    rebuilt = reconstruct(row_codes, codebook)
    segment = lax.slice_in_dim(residual, 0, D // devices * lax.axis_size(("rows", "sub")), axis=1)
    summed = lax.psum_scatter(
        lax.dot_general(
            segment, rebuilt, (((0,), (0,)), ((), ())), preferred_element_type=jnp.float32
        ),
        ("rows", "sub"),
        scatter_dimension=0,
        tiled=True,
    )
    procrustes = summed / jnp.sqrt(jnp.float32(tok_rows * devices))
    column_rotated, column_codes = (
        lax.all_to_all(rotated, "sub", split_axis=1, concat_axis=0, tiled=True),
        lax.all_to_all(row_codes, "sub", split_axis=1, concat_axis=0, tiled=True),
    )
    code_total, counts = subspace_sums(column_rotated, column_codes, codebook.shape[1])
    code_total, counts = (
        lax.psum_scatter(code_total, "rows", scatter_dimension=1, tiled=True),
        lax.psum_scatter(counts, "rows", scatter_dimension=1, tiled=True),
    )
    new_codebook = code_total / (counts[:, :, None] + 1.0)
    return (new_codebook, procrustes)


def solution(mesh):
    placed = (
        P(("rows", "sub"), None),
        P(("rows", "sub")),
        P(),
        P(("rows", "sub"), None),
        P(("rows", "sub"), None),
        P(),
        P(),
    )
    return jax.shard_map(
        per_device,
        mesh=mesh,
        in_specs=placed,
        out_specs=(P("sub", "rows", None), P(("rows", "sub"), None)),
        check_vma=False,
    )
```

profile of v0, /device:TPU:0, one launch (start us, length us, event | category | flops | bytes accessed | tf_op | source)
XLA Modules:
  0.0 972.6 jit_solution(8108674816155765362)
XLA Ops:
  8.0 3.5 gather_fusion
  14.4 11.1 %all-to-all-start.2 = ((s32[128,1,10]{2,1,0:T(1,128)}), s32[128,1,10]{2,1,0:T(1,128)S(1)}, u32[]{:S(2)}, u32[]{:S(2)}) async-start(s32[128,1,10]{2,1,0:T(1,128)} %bitcast.8), calls=%async_computation.2 | async-start | bytes 131072 | tf_op jit(solution)/shard_map/all_to_all | solution.py:81
  30.8 3.9 all-to-all-done.2
  34.6 5.9 all-to-all-start
  40.5 4.0 scatter_custom_fusion.2
  44.6 6.0 reshape.172
  51.8 9.3 all-to-all-start.3
  61.8 11.2 %gather_fusion.1 = bf16[1280,1024]{1,0:T(8,128)(2,1)} fusion(bf16[4096,1024]{1,0:T(8,128)(2,1)} %param.15, s32[2048]{0:T(1024)S(1)} %pad_clamp_fusion), kind=kCustom, calls=%fused_computation.1 | custom fusion | bytes 5248000 | tf_op jit(solution)/shard_map/gather | solution.py:92
  72.9 6.3 reshape.176
  88.2 24.9 %all-to-all-done.3 = bf16[128,10,1024]{2,1,0:T(8,128)(2,1)} async-done(((bf16[128,10,1024]{2,1,0:T(8,128)(2,1)}), bf16[128,10,1024]{2,1,0:T(8,128)(2,1)}, u32[]{:S(2)}, u32[]{:S(2)}) %all-to-all-start.3) | async-done | bytes 2621472 | tf_op jit(solution)/shard_map/all_to_all | solution.py:67
  113.1 3.5 all-to-all-start.1
  116.5 6.6 reshape.175
  123.2 7.9 convolution_convert_fusion
  131.1 4.9 all-to-all-start.4
  136.1 25.4 %while.24 = (s32[]{:T(128)}, bf16[5,256,1024]{2,1,0:T(8,128)(2,1)}, s32[5,256,64]{1,2,0:T(8,128)S(1)}, bf16[64,256,16]{1,2,0:T(8,128)(2,1)S(1)}, s32[]{:T(128)}) while((s32[]{:T(128)}, bf16[5,256,1024]{2,1,0:T(8,128)(2,1)}, s32[5,256,64]{1,2,0:T(8,128)S(1)}, bf16[64,256,16]{1,2,0:T(8,128)(2,1)S(1)}, s32[]{:T(128)}) %tuple.60), condition=%wide.region_12.13_spmd.clone, body=%wide.region_11.12_spmd.clone.sunk | while | flops 138674176 | bytes 3342913 | solution.py:23
  136.1 4.0 fusion.39
  141.2 4.0 fusion.39
  146.3 4.0 fusion.39
  151.3 4.0 fusion.39
  156.4 4.0 fusion.39
  161.9 7.1 select_convert_fusion
  169.0 6.1 convert_element_type.57
  175.1 5.3 copy.42
  180.4 6.9 reshape.173
  187.4 5.2 copy.44
  192.6 47.0 %while.25 = (s32[]{:T(128)}, f32[16,256,16]{1,2,0:T(8,128)S(1)}, f32[16,256]{1,0:T(8,128)S(1)}, s32[10,512,16]{1,0,2:T(8,128)S(1)}, bf16[10,512,16,16]{1,3,2,0:T(8,128)(2,1)}, /*index=5*/s32[]{:T(128)}, s32[]{:T(128)}) while((s32[]{:T(128)}, f32[16,256,16]{1,2,0:T(8,128)S(1)}, f32[16,256]{1,0:T(8,128)S(1)}, ...), condition=%wide.region_8.9_spmd.clone, body=%wide.region_6.8_spmd.clone.sunk | while | flops 77729792 | bytes 1049180 | solution.py:48
  192.6 3.2 fusion.41
  197.3 3.2 fusion.41
  202.0 3.2 fusion.41
  241.7 7.5 fusion.28
  251.1 125.1 %all-reduce = f32[16,256]{1,0:T(8,128)S(1)} all-reduce(f32[16,256]{1,0:T(8,128)S(1)} %get-tuple-element.63), channel_id=3, replica_groups=mesh['rows'=32,'sub'=4] {'rows'}, use_global_device_ids=true, to_apply=%region_10.11.clone | all-reduce | flops 4096 | bytes 32768
  377.8 586.6 %reduce-scatter.6.cloned.1.call-done = f32[8,1024]{1,0:T(8,128)} async-done(((f32[1024,1024]{1,0:T(8,128)}), f32[8,1024]{1,0:T(8,128)}) %reduce-scatter.6.cloned.1.call-update) | async-done | bytes 32784 | tf_op jit(solution)/shard_map/reduce_scatter | solution.py:98
  (128 shorter events, 68.7 us)
Async XLA Ops:
  7.2 116.0 %copy-start = (bf16[1024,1024]{1,0:T(8,128)(2,1)S(1)}, bf16[1024,1024]{1,0:T(8,128)(2,1)}, u32[]{:S(2)}) copy-start(bf16[1024,1024]{1,0:T(8,128)(2,1)} %param.16) | copy-start | bytes 6291460
  14.4 20.3 %all-to-all-start.2 = ((s32[128,1,10]{2,1,0:T(1,128)}), s32[128,1,10]{2,1,0:T(1,128)S(1)}, u32[]{:S(2)}, u32[]{:S(2)}) async-start(s32[128,1,10]{2,1,0:T(1,128)} %bitcast.8), calls=%async_computation.2 | async-start | bytes 131072 | tf_op jit(solution)/shard_map/all_to_all | solution.py:81
  34.6 17.1 %all-to-all-start = ((s32[128,1,640]{2,1,0:T(1,128)}), s32[128,1,640]{2,1,0:T(1,128)S(1)}, u32[]{:S(2)}, u32[]{:S(2)}) async-start(s32[128,1,640]{2,1,0:T(1,128)} %reshape.228), calls=%async_computation | async-start | bytes 655360 | tf_op jit(solution)/shard_map/all_to_all | solution.py:74
  51.8 61.3 %all-to-all-start.3 = ((bf16[128,10,1024]{2,1,0:T(8,128)(2,1)}), bf16[128,10,1024]{2,1,0:T(8,128)(2,1)}, u32[]{:S(2)}, u32[]{:S(2)}) async-start(bf16[128,10,1024]{2,1,0:T(8,128)(2,1)} %reshape.172), calls=%async_computation.3 | async-start | bytes 8388608 | tf_op jit(solution)/shard_map/all_to_all | solution.py:67
  85.1 2.9 copy-start.2
  113.1 18.0 %all-to-all-start.1 = ((s32[1280,4,16]{0,2,1:T(8,128)}), s32[1280,4,16]{0,2,1:T(8,128)S(1)}, u32[]{:S(2)}, u32[]{:S(2)}) async-start(s32[1280,4,16]{0,2,1:T(8,128)} %copy.35), calls=%async_computation.1 | async-start | bytes 655360 | tf_op jit(solution)/shard_map/all_to_all | solution.py:109
  131.1 5.0 copy-start.4
  131.1 44.0 %all-to-all-start.4 = ((bf16[1280,4,256]{0,2,1:T(8,128)(2,1)}), bf16[1280,4,256]{0,2,1:T(8,128)(2,1)}, u32[]{:S(2)}, u32[]{:S(2)}) async-start(bf16[1280,4,256]{0,2,1:T(8,128)(2,1)} %bitcast.65), calls=%async_computation.4 | async-start | bytes 5242880 | tf_op jit(solution)/shard_map/all_to_all | solution.py:108
  136.0 240.2 %reduce-scatter.4.cloned.1.call-start = ((), (), s32[]{:S(2)}) async-start(), calls=%async_computation.7 | async-start | bytes 2162688 | tf_op jit(solution)/shard_map/reduce_scatter | solution.py:113
  187.3 5.2 copy-start.3
  241.6 722.7 %reduce-scatter.6.cloned.1.call-start = ((), (), s32[]{:S(2)}) async-start(), calls=%async_computation.8 | async-start | bytes 4227072 | tf_op jit(solution)/shard_map/reduce_scatter | solution.py:98
  241.6 724.1 %copy-start.1 = (bf16[1024,1024]{1,0:T(8,128)(2,1)S(1)}, bf16[1024,1024]{1,0:T(8,128)(2,1)}, u32[]{:S(2)}) copy-start(bf16[1024,1024]{1,0:T(8,128)(2,1)} %param.16) | copy-start | bytes 6291460
  249.2 0.7 copy-start.5
Sparse Core Ops, SparseCore 0:
  241.7 77.8 reduce-scatter.3
  322.0 642.3 reduce-scatter.5
where the time goes:
time: 975 us; the launch traced here: 973 us
  waiting for transfers between devices  617 us (63%)
  blocking collectives  125 us (13%)
  local copies, waits for them, and re-layouts  86.2 us (9%)
  matrix products  67.3 us (7%)
  starting transfers between devices  34.8 us (4%)
  other arithmetic  27.1 us (3%)
  between operations  14.9 us (2%)
    reduce_scatter x1, waiting for transfers between devices, per_device(): lax.psum_scatter(lax.dot_general(segment, rebuilt, (((0,), (0,)), ((), ()...  587 us
    unnamed x1, blocking collectives  125 us
    dot_general x10, matrix products, accumulate(): jnp.einsum('bmk,bmd->mkd', onehot, segment, preferred_element_type=jnp.fl...  31.9 us
    all_to_all x1, waiting for transfers between devices, per_device(): lax.all_to_all(send_vectors.reshape(devices, capacity, D), ('rows', 'sub'...  24.9 us
    dot_general x5, matrix products, decode_block(): jnp.einsum('bmk,mkd->bmd', onehot, codebook, preferred_element_type=jnp.f...  19.9 us
  transfers between devices with their start and end apart: 7, of which 4 were waited for; matrix products, arithmetic and copies ran while one was open for 11% of the time, Pallas kernels for 0%

commit v1 on v0

v1 whole, which is shorter than its diff:
```python
import jax
import jax.numpy as jnp
from jax import lax
from jax.experimental import pallas as pl
from jax.experimental.pallas import tpu as pltpu
from jax.sharding import PartitionSpec as P

D = 1024
M = 64
K = 256
DS = 16
CAP = 10
SLOT = 16
WIDE = D + 2 * 128 + 128
F32 = jnp.float32
BF = jnp.bfloat16
MESH = pl.DeviceIdType.MESH
VMEM = pltpu.VMEM

PARTS = ((0, 512, "xyz"), (512, 1024, "yzx"), (1024, WIDE, "zxy"))
DIM = {"x": 0, "z": 1, "y": 2}


def local_kernel(v_ref, c_ref, rotation_ref, codes_ref, table_ref, sums_ref, x_ref, reb_ref, hi_ref, lo_ref):
    near = v_ref.shape[0]
    tokens = x_ref.shape[0]
    blocks = tokens // 256
    x_ref[0:near, :] = v_ref[...]
    x_ref[near:tokens, :] = -c_ref[...]

    def decode(m, carry):
        row = codes_ref[pl.ds(m, 1), :]
        for block in range(tokens // 128):
            index = jnp.broadcast_to(row[:, block * 128 : (block + 1) * 128], (8, 128))
            low = index & 127
            halves = []
            for half in range(2):
                start = pl.multiple_of(m * DS + 8 * half, 8)
                first = jnp.take_along_axis(table_ref[pl.ds(start, 8), 0:128], low, axis=1)
                second = jnp.take_along_axis(table_ref[pl.ds(start, 8), 128:256], low, axis=1)
                halves.append(jnp.where(index >= 0, jnp.where(index >= 128, second, first), 0.0))
            reb_ref[pl.ds(pl.multiple_of(m * DS, DS), DS), block * 128 : (block + 1) * 128] = jnp.concatenate(
                halves, 0
            ).astype(BF)
        return carry

    lax.fori_loop(0, M, decode, 0)

    def rotate(i, carry):
        columns = pl.ds(pl.multiple_of(i * 256, 256), 256)
        turned = jnp.dot(x_ref[...], rotation_ref[:, columns], preferred_element_type=F32)
        upper = turned.astype(BF)
        hi_ref[:, columns] = upper
        lo_ref[:, columns] = (turned - upper.astype(F32)).astype(BF)
        return carry

    lax.fori_loop(0, D // 256, rotate, 0)

    def cross(i, carry):
        rows = pl.ds(pl.multiple_of(i * 256, 256), 256)
        block = lax.dot_general(
            x_ref[:, rows], reb_ref[...], (((0,), (1,)), ((), ())), preferred_element_type=F32
        )
        sums_ref[pl.ds(i * 4, 4), :, :, :, 0:D] = block.reshape(4, 2, 4, 8, D)
        return carry

    lax.fori_loop(0, D // 256, cross, 0)

    lane = lax.broadcasted_iota(jnp.int32, (256, 128), 1)
    level = lax.broadcasted_iota(jnp.int32, (K, 256), 0).astype(F32).astype(BF)
    one, zero = jnp.asarray(1, BF), jnp.asarray(0, BF)

    def totals(y, carry):
        counts = jnp.zeros((K, 128), F32)
        for g in range(2):
            columns = pl.ds(pl.multiple_of(y * 256 + g * 128, 128), 128)
            acc = jnp.zeros((K, 256), F32)
            for block in range(blocks):
                span = slice(block * 256, (block + 1) * 256)
                upper, lower = hi_ref[span, columns], lo_ref[span, columns]
                for j in range(8):
                    row = codes_ref[pl.ds(y * 16 + g * 8 + j, 1), span].astype(F32).astype(BF)
                    onehot = jnp.where(row == level, one, zero)
                    mine = lane // DS == j
                    right = jnp.concatenate([jnp.where(mine, upper, zero), jnp.where(mine, lower, zero)], 1)
                    acc = acc + jnp.dot(onehot, right, preferred_element_type=F32)
                    if block * 256 < near:
                        pick = jnp.where(lane == g * 8 + j, one, zero)
                        counts = counts + jnp.dot(onehot, pick, preferred_element_type=F32)
            both = acc[:, :128] + acc[:, 128:]
            sums_ref[:, :, pl.ds(y, 1), :, D + g * 128 : D + (g + 1) * 128] = both.reshape(16, 2, 1, 8, 128)
        sums_ref[:, :, pl.ds(y, 1), :, D + 256 : D + 384] = counts.reshape(16, 2, 1, 8, 128)
        return carry

    lax.fori_loop(0, 4, totals, 0)


def local_sums(vectors, fetched, rotation, codes_t, table):
    tokens = vectors.shape[0] + fetched.shape[0]
    return pl.pallas_call(
        local_kernel,
        out_shape=jax.ShapeDtypeStruct((16, 2, 4, 8, WIDE), F32),
        in_specs=[pl.BlockSpec(memory_space=VMEM)] * 5,
        out_specs=pl.BlockSpec(memory_space=VMEM),
        scratch_shapes=[
            VMEM((tokens, D), BF),
            VMEM((D, tokens), BF),
            VMEM((tokens, D), BF),
            VMEM((tokens, D), BF),
        ],
        compiler_params=pltpu.CompilerParams(vmem_limit_bytes=56 * 2**20),
        name="local_sums",
    )(vectors, fetched, rotation, codes_t, table)


def scatter_kernel(*refs):
    sums_ref, out_ref = refs[:2]
    scratch = refs[2:]
    pair_send, pair_recv, axis_send, axis_recv = scratch[-4:]
    buffers = [scratch[p * 6 : (p + 1) * 6] for p in range(3)]
    r, y = lax.axis_index("rows"), lax.axis_index("sub")
    core, z, x = r % 2, (r // 2) % 4, r // 8
    at = {"x": x, "y": y, "z": z}

    def device(axis, value):
        if axis == "x":
            return (r + (value - x) * 8, y)
        if axis == "z":
            return (r + (value - z) * 2, y)
        return (r, value)

    mate = (r + 1 - 2 * core, y)
    barrier = pltpu.get_barrier_semaphore()
    pl.semaphore_signal(barrier, inc=1, device_id=mate, device_id_type=MESH)
    for axis in "xyz":
        for step in range(1, 4):
            pl.semaphore_signal(
                barrier, inc=1, device_id=device(axis, (at[axis] + step) % 4), device_id_type=MESH
            )
    pl.semaphore_wait(barrier, 10)

    pair = []
    for p, (begin, end, order) in enumerate(PARTS):
        copy = pltpu.make_async_remote_copy(
            src_ref=sums_ref.at[:, 1 - core, :, :, begin:end],
            dst_ref=buffers[p][0],
            send_sem=pair_send.at[p],
            recv_sem=pair_recv.at[p],
            device_id=mate,
            device_id_type=MESH,
        )
        copy.start()
        pair.append(copy)

    def view(ref, dims, axis, index):
        place = tuple(index if d == axis else slice(None) for d in dims)
        return ref.at[place]

    def send(p, stage, source, target, dims, axis):
        copies = []
        for step in range(1, 4):
            peer = (at[axis] + step) % 4
            copy = pltpu.make_async_remote_copy(
                src_ref=view(source, dims, axis, peer),
                dst_ref=target.at[step - 1],
                send_sem=axis_send.at[p, stage, step - 1],
                recv_sem=axis_recv.at[p, stage, step - 1],
                device_id=device(axis, peer),
                device_id_type=MESH,
            )
            copy.start()
            copies.append(copy)
        return copies

    moving = [None] * 3
    for p, (begin, end, order) in enumerate(PARTS):
        got, first = buffers[p][0], buffers[p][1]
        pair[p].wait_recv()

        def add(i, carry, got=got, first=first, begin=begin, end=end):
            first[i // 4, i % 4] = sums_ref[i, core, :, :, begin:end] + got[i]
            return carry

        lax.fori_loop(0, 16, add, 0)
        moving[p] = send(p, 0, first, buffers[p][2], "xzy", order[0])
    sent = []
    for stage in range(1, 4):
        for p, (begin, end, order) in enumerate(PARTS):
            axis = order[stage - 1]
            dims = "".join(d for d in "xzy" if d not in order[: stage - 1])
            rest = dims.replace(axis, "")
            source = (buffers[p][1], buffers[p][3], buffers[p][5])[stage - 1]
            target = (buffers[p][2], buffers[p][4], None)[stage - 1]
            for copy in moving[p]:
                copy.wait_recv()
            sent += moving[p]
            if stage < 3:
                following = (buffers[p][3], buffers[p][5])[stage - 1]
                following[...] = (
                    view(source, dims, axis, at[axis])[...] + target[0] + target[1] + target[2]
                )
                nxt = buffers[p][4] if stage == 1 else last_of(scratch, p)
                moving[p] = send(p, stage, following, nxt, rest, order[stage])
            else:
                landed = last_of(scratch, p)
                out_ref[:, begin:end] = source[at[axis]] + landed[0] + landed[1] + landed[2]
    for copy in pair + sent:
        copy.wait_send()


def last_of(scratch, p):
    return scratch[18 + p]


def scatter_sums(sums):
    scratch = []
    for begin, end, order in PARTS:
        wide = end - begin
        scratch += [
            VMEM((16, 4, 8, wide), F32),
            VMEM((4, 4, 4, 8, wide), F32),
            VMEM((3, 4, 4, 8, wide), F32),
            VMEM((4, 4, 8, wide), F32),
            VMEM((3, 4, 8, wide), F32),
            VMEM((4, 8, wide), F32),
        ]
    for begin, end, order in PARTS:
        scratch.append(VMEM((3, 8, end - begin), F32))
    return pl.pallas_call(
        scatter_kernel,
        out_shape=jax.ShapeDtypeStruct((8, WIDE), F32),
        in_specs=[pl.BlockSpec(memory_space=VMEM)],
        out_specs=pl.BlockSpec(memory_space=VMEM),
        scratch_shapes=scratch
        + [
            pltpu.SemaphoreType.DMA((3,)),
            pltpu.SemaphoreType.DMA((3,)),
            pltpu.SemaphoreType.DMA((3, 3, 3)),
            pltpu.SemaphoreType.DMA((3, 3, 3)),
        ],
        compiler_params=pltpu.CompilerParams(
            collective_id=0, has_side_effects=True, vmem_limit_bytes=56 * 2**20
        ),
        name="scatter_sums",
    )(sums)


def per_device(vectors, coarse_list, list_slot, codes, centroids, rotation, codebook):
    devices = lax.axis_size(("rows", "sub"))
    near = vectors.shape[0]
    list_rows = centroids.shape[0]
    slot_of = list_slot[coarse_list]
    owner_of = slot_of // list_rows
    local_row = slot_of % list_rows
    earlier = jnp.arange(near)[:, None] < jnp.arange(near)[None, :]
    rank = jnp.sum((owner_of[:, None] == owner_of[None, :]) & earlier, axis=0)
    position = owner_of * SLOT + rank
    message = jnp.concatenate(
        [codes + 1, (local_row // 64 + 1)[:, None], (local_row % 64 + 1)[:, None], jnp.zeros((near, 62), jnp.int32)],
        axis=1,
    ).astype(BF)
    place = (jnp.arange(devices * SLOT)[:, None] == position[None, :]).astype(BF)
    outgoing = jnp.dot(place, message, preferred_element_type=F32).astype(BF)
    incoming = lax.all_to_all(
        outgoing.reshape(devices, SLOT, 128), ("rows", "sub"), split_axis=0, concat_axis=0, tiled=True
    )
    arrived = incoming[:, :CAP, :].astype(jnp.int32).transpose(2, 1, 0).reshape(128, CAP * devices) - 1
    row = arrived[M] * 64 + arrived[M + 1]
    fetched = centroids[jnp.maximum(row, 0)]
    codes_t = jnp.concatenate([codes.T, arrived[:M]], axis=1)
    table = codebook.transpose(0, 2, 1).reshape(D, K).astype(F32)
    summed = scatter_sums(local_sums(vectors, fetched, rotation, codes_t, table))
    procrustes = summed[:, :D] / jnp.sqrt(jnp.float32(near * devices))
    code_total = summed[:, D : D + 256].reshape(8, 16, DS).transpose(1, 0, 2)
    counts = summed[:, D + 256 : D + 272].T
    return (code_total / (counts[:, :, None] + 1.0), procrustes)


def solution(mesh):
    placed = (
        P(("rows", "sub"), None),
        P(("rows", "sub")),
        P(),
        P(("rows", "sub"), None),
        P(("rows", "sub"), None),
        P(),
        P(),
    )
    return jax.shard_map(
        per_device,
        mesh=mesh,
        in_specs=placed,
        out_specs=(P("sub", "rows", None), P(("rows", "sub"), None)),
        check_vma=False,
    )
```

time: 975 us -> 120 us (0.12)
  waiting for transfers between devices: 617 us -> 12.1 us
  blocking collectives: 125 us -> 0 us
  Pallas kernels: 0 us -> 71.5 us
  local copies, waits for them, and re-layouts: 86.2 us -> 15.5 us
  matrix products: 67.3 us -> 1.32 us
  starting transfers between devices: 34.8 us -> 11.1 us
  other arithmetic: 27.1 us -> 6.76 us
  between operations: 14.9 us -> 0.77 us
    reduce_scatter x2 -> x0, waiting for transfers between devices: 587 us -> none  [the longest x1 587 us: per_device(): lax.psum_scatter(lax.dot_general(segment, rebuilt, (((0,), (0,)), ((), ()...]
    unnamed x1 -> x0, blocking collectives: 125 us -> none
    pallas_call x0 -> x2, Pallas kernels: none -> 71.5 us  [the longest x1 38.6 us: local_sums(): pl.pallas_call(local_kernel, out_shape=jax.ShapeDtypeStruct((16, 2, 4, 8,...]
    dot_general x17 -> x1, matrix products: 67.3 us -> 1.32 us  [per_device(): outgoing = jnp.dot(place, message, preferred_element_type=F32).astype(BF)]
    all_to_all x5 -> x1, starting transfers between devices: 34.7 us -> 11.1 us  [per_device(): lax.all_to_all(outgoing.reshape(devices, SLOT, 128), ('rows', 'sub'), spl...]
    convert_element_type x3 -> x0, local copies, waits for them, and re-layouts: 19 us -> none  [the longest x2 12.9 us: per_device(): difference = got_vectors.astype(jnp.float32) - fetched.astype(jnp.float32)]
    all_to_all x5 -> x1, waiting for transfers between devices: 30 us -> 12.1 us  [per_device(): lax.all_to_all(outgoing.reshape(devices, SLOT, 128), ('rows', 'sub'), spl...]
    reshape x4 -> x1, local copies, waits for them, and re-layouts: 14.3 us -> 0.08 us  [per_device(): code_total = summed[:, D:D + 256].reshape(8, 16, DS).transpose(1, 0, 2)]
  transfers between devices with their start and end apart: 7 -> 1, of which waited for: 4 -> 1; matrix products, arithmetic and copies ran while one was open for 11% -> 1% of each run, Pallas kernels for 0% -> 0%
where the time goes in v1:
time: 120 us; the launch traced here: 119 us
  Pallas kernels  71.5 us (60%)
  local copies, waits for them, and re-layouts  15.5 us (13%)
  waiting for transfers between devices  12.1 us (10%)
  starting transfers between devices  11.1 us (9%)
  other arithmetic  6.76 us (6%)
  matrix products  1.32 us (1%)
    pallas_call x1, Pallas kernels, local_sums(): pl.pallas_call(local_kernel, out_shape=jax.ShapeDtypeStruct((16, 2, 4, 8,...  38.6 us
    pallas_call x1, Pallas kernels, scatter_sums(): pl.pallas_call(scatter_kernel, out_shape=jax.ShapeDtypeStruct((8, WIDE),...  32.9 us
    all_to_all x1, waiting for transfers between devices, per_device(): lax.all_to_all(outgoing.reshape(devices, SLOT, 128), ('rows', 'sub'), spl...  12.1 us
    gather x1, local copies, waits for them, and re-layouts, per_device(): fetched = centroids[jnp.maximum(row, 0)]  11.2 us
    all_to_all x1, starting transfers between devices, per_device(): lax.all_to_all(outgoing.reshape(devices, SLOT, 128), ('rows', 'sub'), spl...  11.1 us
  transfers between devices with their start and end apart: 1, of which 1 were waited for; matrix products, arithmetic and copies ran while one was open for 1% of the time, Pallas kernels for 0%

profile of v1, /device:TPU:0, one launch (start us, length us, event | category | flops | bytes accessed | tf_op | source)
XLA Modules:
  0.0 119.1 jit_solution(14117692817818146524)
XLA Ops:
  0.6 0.0 copy-start
  0.6 0.0 copy-start.1
  0.7 0.8 compare_select_fusion.2
  1.5 0.7 copy-done
  2.2 1.7 %gather_fusion = s32[256]{0:T(256)S(1)} fusion(s32[524288]{0:T(1024)S(1)} %copy-done, s32[1024]{0:T(1024)S(1)} %pad_clamp_fusion.1), kind=kCustom, calls=%fused_computation | custom fusion | bytes 3072 | tf_op jit(solution)/shard_map/gather | solution.py:252
  4.0 0.1 convert_reduce_fusion
  4.2 0.8 add_convert_fusion
  5.0 0.1 pad.5.clone
  5.1 1.3 %convolution_convert_fusion = bf16[2048,128]{1,0:T(8,128)(2,1)} fusion(s32[256]{0:T(256)S(1)} %multiply_add_fusion, bf16[256,1]{0,1:T(2,128)(2,1)S(1)} %fusion.12, bf16[256,1]{0,1:T(2,128)(2,1)S(1)} %get-tuple-element.2, bf16[256,64]{0,1:T(8,128)(2,1)S(1)} %add_convert_fusion, bf16[128]{0:T(256)(128)(2,1)S(1)} %pad.5.clone), kind=kOutput, calls=%fused_computation.2 | convolution fusion | flops 135266304 | bytes 559360 | tf_op jit(solution)/shard_map/dot_general | solution.py:263
  6.4 11.1 %all-to-all-start = ((bf16[128,16,128]{2,1,0:T(8,128)(2,1)}), bf16[128,16,128]{2,1,0:T(8,128)(2,1)S(1)}, u32[]{:S(2)}, u32[]{:S(2)}) async-start(bf16[128,16,128]{2,1,0:T(8,128)(2,1)} %bitcast.23), calls=%async_computation | async-start | bytes 1048576 | tf_op jit(solution)/shard_map/all_to_all | solution.py:264
  17.6 0.0 copy-done.1
  17.6 1.2 %convert_element_type.25 = f32[64,256,16]{1,2,0:T(8,128)} convert(bf16[64,256,16]{1,2,0:T(8,128)(2,1)S(1)} %copy-done.1) | non-fusion elementwise | flops 262144 | bytes 1572864 | tf_op jit(solution)/shard_map/convert_element_type | solution.py:271
  18.8 0.0 copy-start.2
  18.8 12.1 %all-to-all-done = bf16[128,16,128]{2,1,0:T(8,128)(2,1)S(1)} async-done(((bf16[128,16,128]{2,1,0:T(8,128)(2,1)}), bf16[128,16,128]{2,1,0:T(8,128)(2,1)S(1)}, u32[]{:S(2)}, u32[]{:S(2)}) %all-to-all-start) | async-done | bytes 524320 | tf_op jit(solution)/shard_map/all_to_all | solution.py:264
  30.9 0.7 copy.29
  31.6 0.1 add_bitcast_fusion
  31.8 0.1 copy.33
  32.0 0.0 copy-done.2
  32.0 0.8 pad_add_fusion.codes_ref
  32.7 11.2 %gather_fusion.1 = bf16[1280,1024]{1,0:T(8,128)(2,1)} fusion(bf16[4096,1024]{1,0:T(8,128)(2,1)} %param.11, s32[2048]{0:T(1024)S(1)} %pad_clamp_fusion), kind=kCustom, calls=%fused_computation.1 | custom fusion | bytes 5248000 | tf_op jit(solution)/shard_map/gather | solution.py:269
  43.9 38.6 %local_sums.1.refs_0_ = f32[16,2,4,8,1408]{4,3,2,1,0:T(8,128)} custom-call(bf16[256,1024]{1,0:T(8,128)(2,1)} %v_ref.1, bf16[1280,1024]{1,0:T(8,128)(2,1)} %gather_fusion.1, bf16[1024,1024]{1,0:T(8,128)(2,1)} %rotation_ref.1, s32[64,1536]{1,0:T(8,128)} %pad_add_fusion.codes_ref, f32[1024,256]{1,0:T(8,128)} %bitcast.19), custom_call_target="tpu_custom_call" | custom-call | tf_op jit(solution)/shard_map/local_sums/pallas_call | solution.py:100
  82.5 32.9 %scatter_sums.1 = f32[8,1408]{1,0:T(8,128)} custom-call(f32[16,2,4,8,1408]{4,3,2,1,0:T(8,128)} %local_sums.1.refs_0_), custom_call_target="tpu_custom_call" | custom-call | tf_op jit(solution)/shard_map/scatter_sums/pallas_call | solution.py:229
  115.4 0.7 add_bitcast_fusion.1
  116.1 0.7 slice.31
  116.8 1.4 %slice_multiply_fusion = f32[8,1024]{1,0:T(8,128)} fusion(f32[8,1408]{1,0:T(8,128)} %scatter_sums.1), kind=kLoop, calls=%fused_computation.20 | loop fusion | flops 8192 | bytes 65536 | tf_op jit(solution)/shard_map/div | solution.py:273
  118.2 0.1 copy.28
  118.3 0.1 reshape.205
  118.3 0.7 bitcast_divide_fusion
  (9 shorter events, 0.1 us)
Async XLA Ops:
  0.6 1.6 %copy-start = (s32[524288]{0:T(1024)S(1)}, s32[524288]{0:T(1024)}, u32[]{:S(2)}) copy-start(s32[524288]{0:T(1024)} %param.9) | copy-start | bytes 6291460
  0.6 16.9 %copy-start.1 = (bf16[64,256,16]{1,2,0:T(8,128)(2,1)S(1)}, bf16[64,256,16]{1,2,0:T(8,128)(2,1)}, u32[]{:S(2)}) copy-start(bf16[64,256,16]{1,2,0:T(8,128)(2,1)} %param.13) | copy-start | bytes 1572868
  6.4 24.5 %all-to-all-start = ((bf16[128,16,128]{2,1,0:T(8,128)(2,1)}), bf16[128,16,128]{2,1,0:T(8,128)(2,1)S(1)}, u32[]{:S(2)}, u32[]{:S(2)}) async-start(bf16[128,16,128]{2,1,0:T(8,128)(2,1)} %bitcast.23), calls=%async_computation | async-start | bytes 1048576 | tf_op jit(solution)/shard_map/all_to_all | solution.py:264
  18.8 13.2 %copy-start.2 = (s32[256,64]{0,1:T(8,128)S(1)}, s32[256,64]{0,1:T(8,128)}, u32[]{:S(2)}) copy-start(s32[256,64]{0,1:T(8,128)} %param.10) | copy-start | bytes 196612

commit v2 on v0

v2 whole, which is shorter than its diff:
```python
import jax
import jax.numpy as jnp
from jax import lax
from jax.experimental import pallas as pl
from jax.experimental.pallas import tpu as pltpu
from jax.sharding import PartitionSpec as P

D = 1024
M = 64
K = 256
DS = 16
NEAR = 256
LISTS = 4096
DEVICES = 128
CAP = 10
SLOT = 16
FAR = CAP * DEVICES
CHUNK = 512
F32 = jnp.float32
BF = jnp.bfloat16
I32 = jnp.int32
MESH = pl.DeviceIdType.MESH
VMEM = pltpu.VMEM
ANY = pl.ANY
DMA = pltpu.SemaphoreType.DMA

PARTS = ((0, 384, "x", "zy"), (384, 768, "y", "xz"), (768, 1024, "z", "xy"))
DIMS = "xzy"
NT = (((1,), (1,)), ((), ()))
TT = (((0,), (1,)), ((), ()))


def onehot(row, level):
    return jnp.where(row == level, jnp.asarray(1, BF), jnp.asarray(0, BF))


def iota(shape, dim):
    return lax.broadcasted_iota(I32, shape, dim)


def levels(count, width):
    return iota((count, width), 0).astype(F32).astype(BF)


def drain(ref, semaphore):
    pltpu.make_async_copy(ref, ref, semaphore).wait()


def kernel(
    slot_ref,
    codes_ref,
    book_ref,
    vectors_hbm,
    rotation_hbm,
    centroids_hbm,
    out_book_ref,
    out_cross_ref,
    vectors_ref,
    rotation_ref,
    chunk_ref,
    table_ref,
    wide_ref,
    table_book_ref,
    message_ref,
    arrived_ref,
    arrived_wide_ref,
    near_codes_ref,
    far_codes_ref,
    row_ref,
    row_smem,
    counts_ref,
    near_reb_ref,
    far_reb_ref,
    stage_ref,
    far_x_ref,
    turned_ref,
    cross_ref,
    total_ref,
    cross_half_ref,
    ring_refs,
    cross_plane_ref,
    cross_got_ref,
    total_half_ref,
    total_side_ref,
    total_plane_ref,
    total_got_ref,
    local_sem,
    chunk_sem,
    message_send,
    message_recv,
    cross_core_send,
    cross_core_recv,
    ring_send,
    ring_recv,
    cross_plane_send,
    cross_plane_recv,
    total_core_send,
    total_core_recv,
    total_side_send,
    total_side_recv,
    total_plane_send,
    total_plane_recv,
):
    r, y = lax.axis_index("rows"), lax.axis_index("sub")
    core, z, x = r % 2, (r // 2) % 4, r // 8
    me = r * 4 + y
    at = {"x": x, "y": y, "z": z}

    def device(**place):
        spot = dict(at, **place)
        return ((spot["x"] * 4 + spot["z"]) * 2 + core, spot["y"])

    mate = (r + 1 - 2 * core, y)

    def remote(source, target, send, recv, to):
        return pltpu.make_async_remote_copy(
            src_ref=source, dst_ref=target, send_sem=send, recv_sem=recv, device_id=to, device_id_type=MESH
        )

    barrier = pltpu.get_barrier_semaphore()

    def greet(step, carry):
        other = (me + step) % DEVICES
        pl.semaphore_signal(barrier, inc=1, device_id=(other // 4, other % 4), device_id_type=MESH)
        return carry

    lax.fori_loop(1, DEVICES, greet, 0)

    loads = [
        pltpu.make_async_copy(vectors_hbm, vectors_ref, local_sem.at[0]),
        pltpu.make_async_copy(rotation_hbm, rotation_ref, local_sem.at[1]),
    ]
    for load in loads:
        load.start()

    def chunk_load(i):
        return pltpu.make_async_copy(
            centroids_hbm.at[pl.ds(i * CHUNK, CHUNK)], chunk_ref.at[i % 2], chunk_sem.at[i % 2]
        )

    chunk_load(0).start()
    chunk_load(1).start()

    along = jnp.broadcast_to(slot_ref[...].astype(F32), (NEAR, NEAR))
    down = along.T.astype(I32)
    along = along.astype(I32)
    owner = along // LISTS
    same = (owner == down // LISTS) & (iota((NEAR, NEAR), 0) < iota((NEAR, NEAR), 1))
    rank = jnp.sum(jnp.where(same, 1, 0), axis=0, keepdims=True)
    position = owner[0:1] * SLOT + rank
    wide_ref[...] = jnp.zeros((NEAR, 128), F32)
    wide_ref[:, 0:M] = (codes_ref[...] + 1).astype(F32)
    local_row = down[:, 0:128] % LISTS
    lane = iota((NEAR, 128), 1)
    digits = jnp.where(lane == M, local_row // 64 + 1, jnp.where(lane == M + 1, local_row % 64 + 1, 0))
    tokens = wide_ref[...] + digits.astype(F32)
    near_codes_ref[...] = tokens.T[0:M].astype(I32) - 1

    level32, level128 = levels(32, NEAR), levels(128, NEAR)

    def count(side, carry):
        acc = jnp.zeros((32, 128), F32)
        for j in range(16):
            row = near_codes_ref[pl.ds(side * 16 + j, 1), :]
            upper = onehot((row >> 3).astype(F32).astype(BF), level32)
            lower = onehot(((row & 7) + 8 * j).astype(F32).astype(BF), level128)
            acc = acc + lax.dot_general(upper, lower, NT, preferred_element_type=F32)
        counts_ref[pl.ds(pl.multiple_of(side * 32, 32), 32), :] = acc
        return carry

    lax.fori_loop(0, 4, count, 0)
    column = iota((1, 128), 1)
    count_position = ((column % 32) * 4 + column // 32) * SLOT + CAP
    place_of = jnp.concatenate([position, count_position], axis=1)
    payload = jnp.concatenate([tokens.astype(BF), counts_ref[...].astype(BF)], axis=0)

    def build(i, carry):
        place = jnp.where(iota((256, NEAR + 128), 0) + i * 256 == place_of, 1.0, 0.0).astype(BF)
        rows = jnp.dot(place, payload, preferred_element_type=F32)
        message_ref[pl.ds(i * 16, 16)] = rows.astype(BF).reshape(16, SLOT, 128)
        return carry

    lax.fori_loop(0, DEVICES * SLOT // 256, build, 0)
    pl.semaphore_wait(barrier, DEVICES - 1)

    def post(step, carry):
        other = (me + step) % DEVICES
        remote(
            message_ref.at[other], arrived_ref.at[me], message_send, message_recv, (other // 4, other % 4)
        ).start()
        return carry

    lax.fori_loop(1, DEVICES, post, 0)
    arrived_ref[me] = message_ref[me]

    for i in range(8):
        rows = pl.ds(i * 128, 128)
        table_book_ref[rows, :] = book_ref[rows, :].astype(F32)

    def decode(codes, target, width):
        def step(i, carry):
            for j in range(8):
                m = i * 8 + j
                row = codes[pl.ds(m, 1), :]
                for block in range(width // 128):
                    span = slice(block * 128, (block + 1) * 128)
                    index = jnp.broadcast_to(row[:, span], (8, 128))
                    low, high = index & 127, index >= 128
                    halves = []
                    for half in range(2):
                        start = pl.multiple_of(m * DS + 8 * half, 8)
                        first = jnp.take_along_axis(table_book_ref[pl.ds(start, 8), 0:128], low, axis=1)
                        second = jnp.take_along_axis(table_book_ref[pl.ds(start, 8), 128:256], low, axis=1)
                        halves.append(jnp.where(high, second, first))
                    target[pl.ds(pl.multiple_of(m * DS, DS), DS), span] = jnp.concatenate(halves, 0).astype(BF)
            return carry

        lax.fori_loop(0, M // 8, step, 0)

    def rotate(source, width):
        def step(i, carry):
            columns = pl.ds(pl.multiple_of(i * 256, 256), 256)
            turned = lax.dot_general(rotation_ref[:, columns], source[...], TT, preferred_element_type=F32)
            upper = turned.astype(BF)
            lower = (turned - upper.astype(F32)).astype(BF)
            turned_ref[pl.ds(i * 16, 16), 0:DS, 0:width] = upper.reshape(16, DS, width)
            turned_ref[pl.ds(i * 16, 16), DS : 2 * DS, 0:width] = lower.reshape(16, DS, width)
            return carry

        lax.fori_loop(0, 4, step, 0)

    def group(codes, g, width):
        level = levels(128, width)
        upper, lower = [], []
        for j in range(8):
            row = codes[pl.ds(g * 8 + j, 1), :]
            picked = onehot((row & 127).astype(F32).astype(BF), level)
            high = jnp.broadcast_to((row >> 7).astype(F32).astype(BF), (2 * DS, width))
            values = turned_ref[g * 8 + j, :, 0:width]
            zero = jnp.zeros_like(values)
            masked = jnp.concatenate(
                [jnp.where(high == jnp.asarray(0, BF), values, zero), jnp.where(high == jnp.asarray(1, BF), values, zero)],
                0,
            )
            both = lax.dot_general(masked, picked, NT, preferred_element_type=F32)
            lower.append(both[0:16] + both[16:32])
            upper.append(both[32:48] + both[48:64])
        return jnp.concatenate(lower, 0).T, jnp.concatenate(upper, 0).T

    loads[0].wait()
    loads[1].wait()
    decode(near_codes_ref, near_reb_ref, NEAR)

    def near_cross(i, carry):
        columns = pl.ds(pl.multiple_of(i * 256, 256), 256)
        block = lax.dot_general(vectors_ref[:, columns], near_reb_ref[...], TT, preferred_element_type=F32)
        cross_ref[i] = block.reshape(4, 2, 4, 8, D)
        return carry

    lax.fori_loop(0, 4, near_cross, 0)
    rotate(vectors_ref, NEAR)

    def near_total(g, carry):
        lower, upper = group(near_codes_ref, g, NEAR)
        total_ref[g % 2, 0:2, :, :, g // 2] = lower.reshape(2, 4, 2, 8, 128)
        total_ref[g % 2, 2:4, :, :, g // 2] = upper.reshape(2, 4, 2, 8, 128)
        return carry

    lax.fori_loop(0, 8, near_total, 0)

    def widen(i, carry):
        chunk_load(i).wait()

        def part(k, inner):
            source = chunk_ref.at[i % 2]
            for c in range(8):
                piece = source[pl.ds(pl.multiple_of(k * 16, 16), 16), c * 128 : (c + 1) * 128].astype(F32)
                start = pl.multiple_of((i * (CHUNK // 16) + k) * 128 + c * 8, 8)
                table_ref[pl.ds(start, 8), :] = piece[0:8]
                table_ref[pl.ds(pl.multiple_of(start + 64, 8), 8), :] = piece[8:16]
            return inner

        lax.fori_loop(0, CHUNK // 16, part, 0)

        @pl.when(i + 2 < LISTS // CHUNK)
        def _():
            chunk_load(i + 2).start()

        return carry

    lax.fori_loop(0, LISTS // CHUNK, widen, 0)
    table_ref[LISTS * 8 : LISTS * 8 + 64, :] = jnp.zeros((64, 128), F32)

    drain(arrived_ref.at[pl.ds(0, DEVICES - 1)], message_recv)
    for i in range(8):
        arrived_wide_ref[i * 256 : (i + 1) * 256] = arrived_ref[i * 16 : (i + 1) * 16].astype(F32).reshape(256, 128)
    for j in range(CAP):
        turned_over = arrived_wide_ref[pl.ds(j, DEVICES, stride=SLOT), :].T.astype(I32) - 1
        far_codes_ref[:, j * 128 : (j + 1) * 128] = turned_over[0:M]
        upper, lower = turned_over[M : M + 1], turned_over[M + 1 : M + 2]
        row_ref[j : j + 1, :] = jnp.clip(jnp.where(upper < 0, LISTS, upper * 64 + lower), 0, LISTS)
    for j in range(CAP, 16):
        row_ref[j : j + 1, :] = jnp.zeros((1, 128), I32)
    counted = jnp.sum(arrived_wide_ref[pl.ds(CAP, DEVICES, stride=SLOT), :], axis=0, keepdims=True)
    fetch = pltpu.make_async_copy(row_ref, row_smem, local_sem.at[2])
    fetch.start()
    decode(far_codes_ref, far_reb_ref, FAR)
    fetch.wait()

    def gather(j, carry):
        def take(k, inner):
            for s in range(8):
                row = row_smem[j, k * 8 + s]
                piece = table_ref[pl.ds((row // 8) * 64 + row % 8, 8, stride=8), :]
                stage_ref[pl.ds(k * 64 + s, 8, stride=8), :] = piece
            return inner

        lax.fori_loop(0, 16, take, 0)
        block = stage_ref[...].reshape(16, 8, 8, 128)
        for c in range(8):
            far_x_ref[pl.ds(pl.multiple_of(j * 128, 128), 128), c * 128 : (c + 1) * 128] = (
                -block[:, c].reshape(128, 128)
            ).astype(BF)
        return carry

    lax.fori_loop(0, CAP, gather, 0)

    def cross_core(i):
        return remote(
            cross_ref.at[i, :, 1 - core],
            cross_half_ref.at[i],
            cross_core_send.at[i],
            cross_core_recv.at[i],
            mate,
        )

    def far_cross(i, carry):
        columns = pl.ds(pl.multiple_of(i * 256, 256), 256)
        block = lax.dot_general(far_x_ref[:, columns], far_reb_ref[...], TT, preferred_element_type=F32)
        cross_ref[i] += block.reshape(4, 2, 4, 8, D)
        cross_core(i).start()
        return carry

    lax.fori_loop(0, 4, far_cross, 0)
    rotate(far_x_ref, FAR)

    def join(i, carry):
        cross_core(i).wait_recv()
        cross_half_ref[i] += cross_ref[i, :, core]
        return carry

    lax.fori_loop(0, 4, join, 0)

    def slab(p, value, half):
        begin, end, axis, _ = PARTS[p]
        rest = [d for d in DIMS if d != axis]
        index = []
        for d in DIMS:
            if d == axis:
                index.append(value)
            elif d == rest[0]:
                index.append(pl.ds(half * 2, 2))
            else:
                index.append(slice(None))
        return cross_half_ref.at[tuple(index) + (slice(None), slice(begin, end))]

    def ring(p, slot, value, half, way):
        axis = PARTS[p][2]
        return remote(
            slab(p, value, half),
            ring_refs[p].at[slot],
            ring_send.at[p, slot],
            ring_recv.at[p, slot],
            device(**{axis: (at[axis] + way) % 4}),
        )

    def around(p):
        here = at[PARTS[p][2]]
        return here, (here + 1) % 4, (here + 2) % 4, (here + 3) % 4

    first, second = [], []
    for p in range(3):
        here, after, beyond, before = around(p)
        copies = [
            ring(p, 0, beyond, 0, 1),
            ring(p, 1, beyond, 1, 3),
            ring(p, 2, after, 1, 1),
            ring(p, 3, before, 0, 3),
        ]
        for copy in copies:
            copy.start()
        first.append(copies)

    def side(q):
        return (y + 1 + q) % 4

    def total_core(q):
        return remote(
            total_ref.at[:, :, :, 1 - core, side(q)],
            total_half_ref.at[q],
            total_core_send.at[q],
            total_core_recv.at[q],
            mate,
        )

    def total_side(q):
        return remote(
            total_half_ref.at[q],
            total_side_ref.at[q],
            total_side_send.at[q],
            total_side_recv.at[q],
            (r, side(q)),
        )

    def far_total(q):
        def step(half, carry):
            lower, upper = group(far_codes_ref, side(q) * 2 + half, FAR)
            total_ref[half, 0:2, :, :, side(q)] += lower.reshape(2, 4, 2, 8, 128)
            total_ref[half, 2:4, :, :, side(q)] += upper.reshape(2, 4, 2, 8, 128)
            return carry

        lax.fori_loop(0, 2, step, 0)
        total_core(q).start()

    def pass_on(q):
        total_core(q).wait_recv()
        total_half_ref[q] += total_ref[:, :, :, core, side(q)]
        if q < 3:
            total_side(q).start()

    far_total(0)
    far_total(1)
    pass_on(0)
    for p in range(3):
        here, after, beyond, before = around(p)
        first[p][0].wait_recv()
        target = slab(p, after, 0)
        target[...] += ring_refs[p][0]
        first[p][1].wait_recv()
        target = slab(p, before, 1)
        target[...] += ring_refs[p][1]
        copies = [ring(p, 4, after, 0, 1), ring(p, 5, before, 1, 3)]
        for copy in copies:
            copy.start()
        second.append(copies)
    far_total(2)
    pass_on(1)
    far_total(3)
    pass_on(2)

    def plane_lanes(p):
        return slice(PARTS[p][0], PARTS[p][1])

    def cross_plane(p, step):
        axes = PARTS[p][3]
        i, j = (at[axes[0]] + step // 4) % 4, (at[axes[1]] + step % 4) % 4
        return remote(
            cross_plane_ref.at[i, j, :, plane_lanes(p)],
            cross_got_ref.at[step, :, plane_lanes(p)],
            cross_plane_send.at[p],
            cross_plane_recv.at[p],
            device(**{axes[0]: i, axes[1]: j}),
        )

    for p in range(3):
        here = around(p)[0]
        for copy in first[p][2:] + second[p]:
            copy.wait_recv()
        got = ring_refs[p]
        cross_plane_ref[0:2, :, :, plane_lanes(p)] = slab(p, here, 0)[...] + got[3] + got[4]
        cross_plane_ref[2:4, :, :, plane_lanes(p)] = slab(p, here, 1)[...] + got[2] + got[5]

        def spread(step, carry, p=p):
            cross_plane(p, step).start()
            return carry

        lax.fori_loop(1, 16, spread, 0)

    pass_on(3)
    for q in range(3):
        total_side(q).wait_recv()
    total_plane_ref[...] = total_half_ref[3] + total_side_ref[0] + total_side_ref[1] + total_side_ref[2]

    def total_plane(step):
        i, j = (x + step // 4) % 4, (z + step % 4) % 4
        return remote(
            total_plane_ref.at[:, i, j],
            total_got_ref.at[step],
            total_plane_send,
            total_plane_recv,
            device(x=i, z=j),
        )

    def spread_total(step, carry):
        total_plane(step).start()
        return carry

    lax.fori_loop(1, 16, spread_total, 0)

    for p in range(3):
        axes = PARTS[p][3]
        drain(cross_got_ref.at[pl.ds(1, 15), :, plane_lanes(p)], cross_plane_recv.at[p])
        acc = cross_plane_ref[at[axes[0]], at[axes[1]], :, plane_lanes(p)]
        for step in range(1, 16):
            acc = acc + cross_got_ref[step, :, plane_lanes(p)]
        out_cross_ref[:, plane_lanes(p)] = acc / jnp.sqrt(jnp.float32(NEAR * DEVICES))
    drain(total_got_ref.at[pl.ds(1, 15)], total_plane_recv)
    spread_counts = jnp.broadcast_to(counted, (8, 128))
    for half in range(2):
        acc = total_plane_ref[half, x, z]
        for step in range(1, 16):
            acc = acc + total_got_ref[step, half]
        where = (half * 8 + iota((8, 128), 1) // DS) * 8 + iota((8, 128), 0)
        mean = acc / (jnp.take_along_axis(spread_counts, where, axis=1) + 1.0)
        for j in range(8):
            out_book_ref[half * 8 + j] = mean[:, j * DS : (j + 1) * DS]

    drain(message_ref.at[pl.ds(0, DEVICES - 1)], message_send)

    def left(i, carry):
        cross_core(i).wait_send()
        return carry

    lax.fori_loop(0, 4, left, 0)
    for p in range(3):
        for copy in first[p] + second[p]:
            copy.wait_send()
        drain(cross_got_ref.at[pl.ds(1, 15), :, plane_lanes(p)], cross_plane_send.at[p])
    for q in range(4):
        total_core(q).wait_send()
        if q < 3:
            total_side(q).wait_send()
    drain(total_got_ref.at[pl.ds(1, 15)], total_plane_send)


def per_device(vectors, coarse_list, list_slot, codes, centroids, rotation, codebook):
    slot_of = list_slot[coarse_list].reshape(1, NEAR)
    book = codebook.transpose(0, 2, 1).reshape(D, K)
    here = pl.BlockSpec(memory_space=VMEM)
    away = pl.BlockSpec(memory_space=ANY)
    return pl.pallas_call(
        kernel,
        out_shape=(jax.ShapeDtypeStruct((16, 8, DS), F32), jax.ShapeDtypeStruct((8, D), F32)),
        in_specs=[here, here, here, away, away, away],
        out_specs=(here, here),
        scratch_shapes=[
            VMEM((NEAR, D), BF),
            VMEM((D, D), BF),
            VMEM((2, CHUNK, D), BF),
            VMEM((LISTS * 8 + 64, 128), F32),
            VMEM((NEAR, 128), F32),
            VMEM((D, K), F32),
            VMEM((DEVICES, SLOT, 128), BF),
            VMEM((DEVICES, SLOT, 128), BF),
            VMEM((DEVICES * SLOT, 128), F32),
            VMEM((M, NEAR), I32),
            VMEM((M, FAR), I32),
            VMEM((16, 128), I32),
            pltpu.SMEM((16, 128), I32),
            VMEM((128, 128), F32),
            VMEM((D, NEAR), BF),
            VMEM((D, FAR), BF),
            VMEM((1024, 128), F32),
            VMEM((FAR, D), BF),
            VMEM((M, 2 * DS, FAR), BF),
            VMEM((4, 4, 2, 4, 8, D), F32),
            VMEM((2, 4, 4, 2, 4, 8, 128), F32),
            VMEM((4, 4, 4, 8, D), F32),
            [VMEM((6, 2, 4, 8, end - begin), F32) for begin, end, _, _ in PARTS],
            VMEM((4, 4, 8, D), F32),
            VMEM((16, 8, D), F32),
            VMEM((4, 2, 4, 4, 8, 128), F32),
            VMEM((3, 2, 4, 4, 8, 128), F32),
            VMEM((2, 4, 4, 8, 128), F32),
            VMEM((16, 2, 8, 128), F32),
            DMA((3,)),
            DMA((2,)),
            DMA,
            DMA,
            DMA((4,)),
            DMA((4,)),
            DMA((3, 6)),
            DMA((3, 6)),
            DMA((3,)),
            DMA((3,)),
            DMA((4,)),
            DMA((4,)),
            DMA((3,)),
            DMA((3,)),
            DMA,
            DMA,
        ],
        compiler_params=pltpu.CompilerParams(
            collective_id=0, has_side_effects=True, vmem_limit_bytes=56 * 2**20
        ),
        name="refine",
    )(slot_of, codes, book, vectors, rotation, centroids)


def solution(mesh):
    placed = (
        P(("rows", "sub"), None),
        P(("rows", "sub")),
        P(),
        P(("rows", "sub"), None),
        P(("rows", "sub"), None),
        P(),
        P(),
    )
    return jax.shard_map(
        per_device,
        mesh=mesh,
        in_specs=placed,
        out_specs=(P("sub", "rows", None), P(("rows", "sub"), None)),
        check_vma=False,
    )
```

time: 975 us -> 84.7 us (0.09)
  waiting for transfers between devices: 617 us -> 0 us
  blocking collectives: 125 us -> 0 us
  local copies, waits for them, and re-layouts: 86.2 us -> 7.5 us
  Pallas kernels: 0 us -> 75.3 us
  matrix products: 67.3 us -> 0 us
  starting transfers between devices: 34.8 us -> 0 us
  other arithmetic: 27.1 us -> 0.84 us
  between operations: 14.9 us -> 0.65 us
    reduce_scatter x2 -> x0, waiting for transfers between devices: 587 us -> none  [the longest x1 587 us: per_device(): lax.psum_scatter(lax.dot_general(segment, rebuilt, (((0,), (0,)), ((), ()...]
    unnamed x1 -> x0, blocking collectives: 125 us -> none
    pallas_call x0 -> x1, Pallas kernels: none -> 75.3 us  [per_device(): pl.pallas_call(kernel, out_shape=(jax.ShapeDtypeStruct((16, 8, DS), F32),...]
    dot_general x17 -> x0, matrix products: 67.3 us -> none  [the longest x10 31.9 us: accumulate(): jnp.einsum('bmk,bmd->mkd', onehot, segment, preferred_element_type=jnp.fl...]
    all_to_all x5 -> x0, starting transfers between devices: 34.7 us -> none  [the longest x1 11.1 us: per_device(): lax.all_to_all(send_rows.reshape(devices, capacity), ('rows', 'sub'), spl...]
    all_to_all x5 -> x0, waiting for transfers between devices: 30 us -> none  [the longest x1 24.9 us: per_device(): lax.all_to_all(send_vectors.reshape(devices, capacity, D), ('rows', 'sub'...]
    convert_element_type x3 -> x0, local copies, waits for them, and re-layouts: 19 us -> none  [the longest x2 12.9 us: per_device(): difference = got_vectors.astype(jnp.float32) - fetched.astype(jnp.float32)]
    reduce_sum x11 -> x0, other arithmetic: 14.3 us -> none  [the longest x10 14.1 us: accumulate(): counts = running[1] + jnp.sum(onehot.astype(jnp.float32), axis=0)]
  transfers between devices with their start and end apart: 7 -> 0, of which waited for: 4 -> 0; matrix products, arithmetic and copies ran while one was open for 11% -> 0% of each run, Pallas kernels for 0% -> 0%
where the time goes in v2:
time: 84.7 us; the launch traced here: 84.3 us
  Pallas kernels  75.3 us (89%)
  local copies, waits for them, and re-layouts  7.5 us (9%)
    pallas_call x1, Pallas kernels, per_device(): pl.pallas_call(kernel, out_shape=(jax.ShapeDtypeStruct((16, 8, DS), F32),...  75.3 us
    unnamed x5, local copies, waits for them, and re-layouts  5.19 us
    gather x1, local copies, waits for them, and re-layouts, per_device(): slot_of = list_slot[coarse_list].reshape(1, NEAR)  2.31 us

profile of v2, /device:TPU:0, one launch (start us, length us, event | category | flops | bytes accessed | tf_op | source)
XLA Modules:
  0.0 84.3 jit_solution(9903073644936799313)
XLA Ops:
  0.6 0.0 copy-start
  0.6 0.8 compare_select_fusion
  1.5 0.8 copy-done
  2.2 2.3 %gather_fusion = s32[256]{0:T(256)} fusion(s32[524288]{0:T(1024)S(1)} %copy-done, s32[1024]{0:T(1024)S(1)} %pad_clamp_fusion), kind=kCustom, calls=%fused_computation | custom fusion | bytes 3072 | tf_op jit(solution)/shard_map/gather | solution.py:537
  4.6 1.6 %copy.10.codes_ref = s32[256,64]{1,0:T(8,128)} copy(s32[256,64]{0,1:T(8,128)} %param.10) | data formatting | bytes 131072 | tf_op args[3]
  6.1 75.3 %refine.1 = (f32[16,8,16]{2,1,0:T(8,128)}, f32[8,1024]{1,0:T(8,128)}) custom-call(s32[1,256]{1,0:T(1,128)} %bitcast.5, s32[256,64]{1,0:T(8,128)} %copy.10.codes_ref, bf16[1024,256]{1,0:T(8,128)(2,1)} %bitcast.4, bf16[256,1024]{1,0:T(8,128)(2,1)} %vectors_hbm.1, bf16[1024,1024]{1,0:T(8,128)(2,1)} %rotation_hbm.1, bf16[4096,1024]{1,0:T(8,128)(2,1)} %centroids_hbm.1), custom_call_target="tpu_custom_call" | custom-call | tf_op jit(solution)/shard_map/refine/pallas_call | solution.py:541
  81.5 1.5 %copy.13 = f32[16,8,16]{2,1,0:T(8,128)} copy(f32[16,8,16]{2,1,0:T(8,128)} %get-tuple-element.4) | data formatting | bytes 16384
  83.0 1.4 %copy.14 = f32[8,1024]{1,0:T(8,128)} copy(f32[8,1024]{1,0:T(8,128)} %get-tuple-element.5) | data formatting | bytes 65536
  (1 shorter events, 0.0 us)
Async XLA Ops:
  0.6 1.6 %copy-start = (s32[524288]{0:T(1024)S(1)}, s32[524288]{0:T(1024)}, u32[]{:S(2)}) copy-start(s32[524288]{0:T(1024)} %param.9) | copy-start | bytes 6291460

commit v3 on v2

--- a/solution.py
+++ b/solution.py
@@ -47,24 +47,27 @@
 
 
 def kernel(
-    slot_ref,
-    codes_ref,
+    coarse_smem,
+    coarse_ref,
+    near_codes_ref,
     book_ref,
+    slots_hbm,
     vectors_hbm,
     rotation_hbm,
     centroids_hbm,
-    out_book_ref,
+    out_total_ref,
+    out_counts_ref,
     out_cross_ref,
+    slots_ref,
+    picked_ref,
     vectors_ref,
     rotation_ref,
     chunk_ref,
     table_ref,
-    wide_ref,
     table_book_ref,
     message_ref,
     arrived_ref,
     arrived_wide_ref,
-    near_codes_ref,
     far_codes_ref,
     row_ref,
     row_smem,
@@ -102,7 +105,7 @@
     total_plane_recv,
 ):
     r, y = lax.axis_index("rows"), lax.axis_index("sub")
-    core, z, x = r % 2, (r // 2) % 4, r // 8
+    core, z, x = lax.rem(r, 2), lax.rem(lax.div(r, 2), 4), lax.div(r, 8)
     me = r * 4 + y
     at = {"x": x, "y": y, "z": z}
 
@@ -117,60 +120,81 @@
             src_ref=source, dst_ref=target, send_sem=send, recv_sem=recv, device_id=to, device_id_type=MESH
         )
 
+    def others(dr, first):
+        there = lax.rem(r + dr, DEVICES // 4)
+        return [(there, lax.rem(y + dy, 4)) for dy in range(first, 4)]
+
     barrier = pltpu.get_barrier_semaphore()
 
-    def greet(step, carry):
-        other = (me + step) % DEVICES
-        pl.semaphore_signal(barrier, inc=1, device_id=(other // 4, other % 4), device_id_type=MESH)
-        return carry
-
-    lax.fori_loop(1, DEVICES, greet, 0)
+    def greet(dr, first):
+        for other in others(dr, first):
+            pl.semaphore_signal(barrier, inc=1, device_id=other, device_id_type=MESH)
 
     loads = [
         pltpu.make_async_copy(vectors_hbm, vectors_ref, local_sem.at[0]),
         pltpu.make_async_copy(rotation_hbm, rotation_ref, local_sem.at[1]),
     ]
+    slots_load = pltpu.make_async_copy(slots_hbm, slots_ref, local_sem.at[3])
+    slots_load.start()
+    greet(0, 1)
+
+    level32, level128 = levels(32, NEAR), levels(128, NEAR)
+    counts_ref[...] = jnp.zeros((128, 128), F32)
+
+    def count(i):
+        acc = jnp.zeros((32, 128), F32)
+        for j in range(2):
+            m = i * 2 + j
+            row = near_codes_ref[pl.ds(m, 1), :]
+            upper = onehot((row >> 3).astype(F32).astype(BF), level32)
+            lower = onehot(((row & 7) + 8 * lax.rem(m, 16)).astype(F32).astype(BF), level128)
+            acc = acc + lax.dot_general(upper, lower, NT, preferred_element_type=F32)
+        counts_ref[pl.ds(pl.multiple_of(lax.div(i, 8) * 32, 32), 32), :] += acc
+
+    def greet_and_count(dr, carry):
+        greet(dr, 0)
+        count(dr)
+        return carry
+
+    lax.fori_loop(1, 32, greet_and_count, 0)
+    count(0)
+
+    slots_load.wait()
     for load in loads:
         load.start()
 
     def chunk_load(i):
         return pltpu.make_async_copy(
-            centroids_hbm.at[pl.ds(i * CHUNK, CHUNK)], chunk_ref.at[i % 2], chunk_sem.at[i % 2]
+            centroids_hbm.at[pl.ds(i * CHUNK, CHUNK)], chunk_ref.at[lax.rem(i, 2)], chunk_sem.at[lax.rem(i, 2)]
         )
 
     chunk_load(0).start()
     chunk_load(1).start()
 
-    along = jnp.broadcast_to(slot_ref[...].astype(F32), (NEAR, NEAR))
-    down = along.T.astype(I32)
-    along = along.astype(I32)
-    owner = along // LISTS
-    same = (owner == down // LISTS) & (iota((NEAR, NEAR), 0) < iota((NEAR, NEAR), 1))
+    def look_up(i, carry):
+        for s in range(16):
+            line = coarse_smem[i * 16 + s] >> 7
+            picked_ref[pl.ds(i * 16 + s, 1), :] = slots_ref[pl.ds(line, 1), :]
+        return carry
+
+    lax.fori_loop(0, NEAR // 16, look_up, 0)
+    coarse = jnp.broadcast_to(coarse_ref[...].astype(F32), (128, NEAR)).T.astype(I32)
+    mine = iota((NEAR, 128), 1) == (coarse & 127)
+    slot = jnp.sum(jnp.where(mine, picked_ref[...].astype(F32), 0.0), axis=1, keepdims=True)
+    down = jnp.broadcast_to(slot, (NEAR, NEAR))
+    along = down.T.astype(I32)
+    down = down.astype(I32)
+
+    owner = along >> 12
+    same = (owner == (down >> 12)) & (iota((NEAR, NEAR), 0) < iota((NEAR, NEAR), 1))
     rank = jnp.sum(jnp.where(same, 1, 0), axis=0, keepdims=True)
     position = owner[0:1] * SLOT + rank
-    wide_ref[...] = jnp.zeros((NEAR, 128), F32)
-    wide_ref[:, 0:M] = (codes_ref[...] + 1).astype(F32)
-    local_row = down[:, 0:128] % LISTS
-    lane = iota((NEAR, 128), 1)
-    digits = jnp.where(lane == M, local_row // 64 + 1, jnp.where(lane == M + 1, local_row % 64 + 1, 0))
-    tokens = wide_ref[...] + digits.astype(F32)
-    near_codes_ref[...] = tokens.T[0:M].astype(I32) - 1
-
-    level32, level128 = levels(32, NEAR), levels(128, NEAR)
-
-    def count(side, carry):
-        acc = jnp.zeros((32, 128), F32)
-        for j in range(16):
-            row = near_codes_ref[pl.ds(side * 16 + j, 1), :]
-            upper = onehot((row >> 3).astype(F32).astype(BF), level32)
-            lower = onehot(((row & 7) + 8 * j).astype(F32).astype(BF), level128)
-            acc = acc + lax.dot_general(upper, lower, NT, preferred_element_type=F32)
-        counts_ref[pl.ds(pl.multiple_of(side * 32, 32), 32), :] = acc
-        return carry
-
-    lax.fori_loop(0, 4, count, 0)
+    local_row = along[0:M] & (LISTS - 1)
+    line = iota((M, NEAR), 0)
+    digits = jnp.where(line == 0, (local_row >> 6) + 1, jnp.where(line == 1, (local_row & 63) + 1, 0))
+    tokens = jnp.concatenate([near_codes_ref[...] + 1, digits], axis=0).astype(F32).T
     column = iota((1, 128), 1)
-    count_position = ((column % 32) * 4 + column // 32) * SLOT + CAP
+    count_position = ((column & 31) * 4 + (column >> 5)) * SLOT + CAP
     place_of = jnp.concatenate([position, count_position], axis=1)
     payload = jnp.concatenate([tokens.astype(BF), counts_ref[...].astype(BF)], axis=0)
 
@@ -183,14 +207,19 @@
     lax.fori_loop(0, DEVICES * SLOT // 256, build, 0)
     pl.semaphore_wait(barrier, DEVICES - 1)
 
-    def post(step, carry):
-        other = (me + step) % DEVICES
-        remote(
-            message_ref.at[other], arrived_ref.at[me], message_send, message_recv, (other // 4, other % 4)
-        ).start()
-        return carry
-
-    lax.fori_loop(1, DEVICES, post, 0)
+    def post(dr, first):
+        for other in others(dr, first):
+            remote(
+                message_ref.at[other[0] * 4 + other[1]], arrived_ref.at[me], message_send, message_recv, other
+            ).start()
+
+    post(0, 1)
+
+    def post_row(dr, carry):
+        post(dr, 0)
+        return carry
+
+    lax.fori_loop(1, DEVICES // 4, post_row, 0)
     arrived_ref[me] = message_ref[me]
 
     for i in range(8):
@@ -272,7 +301,7 @@
         chunk_load(i).wait()
 
         def part(k, inner):
-            source = chunk_ref.at[i % 2]
+            source = chunk_ref.at[lax.rem(i, 2)]
             for c in range(8):
                 piece = source[pl.ds(pl.multiple_of(k * 16, 16), 16), c * 128 : (c + 1) * 128].astype(F32)
                 start = pl.multiple_of((i * (CHUNK // 16) + k) * 128 + c * 8, 8)
@@ -298,7 +327,8 @@
         turned_over = arrived_wide_ref[pl.ds(j, DEVICES, stride=SLOT), :].T.astype(I32) - 1
         far_codes_ref[:, j * 128 : (j + 1) * 128] = turned_over[0:M]
         upper, lower = turned_over[M : M + 1], turned_over[M + 1 : M + 2]
-        row_ref[j : j + 1, :] = jnp.clip(jnp.where(upper < 0, LISTS, upper * 64 + lower), 0, LISTS)
+        row = jnp.clip(jnp.where(upper < 0, LISTS, upper * 64 + lower), 0, LISTS)
+        row_ref[j : j + 1, :] = (row >> 3) * 64 + (row & 7)
     for j in range(CAP, 16):
         row_ref[j : j + 1, :] = jnp.zeros((1, 128), I32)
     counted = jnp.sum(arrived_wide_ref[pl.ds(CAP, DEVICES, stride=SLOT), :], axis=0, keepdims=True)
@@ -309,13 +339,12 @@
 
     def gather(j, carry):
         def take(k, inner):
-            for s in range(8):
-                row = row_smem[j, k * 8 + s]
-                piece = table_ref[pl.ds((row // 8) * 64 + row % 8, 8, stride=8), :]
-                stage_ref[pl.ds(k * 64 + s, 8, stride=8), :] = piece
+            pieces = [table_ref[pl.ds(row_smem[j, k * 16 + s], 8, stride=8), :] for s in range(16)]
+            for s in range(16):
+                stage_ref[pl.ds(k * 128 + (s // 8) * 64 + s % 8, 8, stride=8), :] = pieces[s]
             return inner
 
-        lax.fori_loop(0, 16, take, 0)
+        lax.fori_loop(0, 8, take, 0)
         block = stage_ref[...].reshape(16, 8, 8, 128)
         for c in range(8):
             far_x_ref[pl.ds(pl.multiple_of(j * 128, 128), 128), c * 128 : (c + 1) * 128] = (
@@ -371,12 +400,12 @@
             ring_refs[p].at[slot],
             ring_send.at[p, slot],
             ring_recv.at[p, slot],
-            device(**{axis: (at[axis] + way) % 4}),
+            device(**{axis: lax.rem(at[axis] + way, 4)}),
         )
 
     def around(p):
         here = at[PARTS[p][2]]
-        return here, (here + 1) % 4, (here + 2) % 4, (here + 3) % 4
+        return here, lax.rem(here + 1, 4), lax.rem(here + 2, 4), lax.rem(here + 3, 4)
 
     first, second = [], []
     for p in range(3):
@@ -392,7 +421,7 @@
         first.append(copies)
 
     def side(q):
-        return (y + 1 + q) % 4
+        return lax.rem(y + 1 + q, 4)
 
     def total_core(q):
         return remote(
@@ -451,16 +480,27 @@
     def plane_lanes(p):
         return slice(PARTS[p][0], PARTS[p][1])
 
-    def cross_plane(p, step):
+    def spread(start):
+        for j in range(1, 4):
+            start(0, j)
+
+        def row(i, carry):
+            for j in range(4):
+                start(i, j)
+            return carry
+
+        lax.fori_loop(1, 4, row, 0)
+
+    def cross_plane(p, di, dj):
         axes = PARTS[p][3]
-        i, j = (at[axes[0]] + step // 4) % 4, (at[axes[1]] + step % 4) % 4
-        return remote(
+        i, j = lax.rem(at[axes[0]] + di, 4), lax.rem(at[axes[1]] + dj, 4)
+        remote(
             cross_plane_ref.at[i, j, :, plane_lanes(p)],
-            cross_got_ref.at[step, :, plane_lanes(p)],
+            cross_got_ref.at[di * 4 + dj, :, plane_lanes(p)],
             cross_plane_send.at[p],
             cross_plane_recv.at[p],
             device(**{axes[0]: i, axes[1]: j}),
-        )
+        ).start()
 
     for p in range(3):
         here = around(p)[0]
@@ -469,51 +509,38 @@
         got = ring_refs[p]
         cross_plane_ref[0:2, :, :, plane_lanes(p)] = slab(p, here, 0)[...] + got[3] + got[4]
         cross_plane_ref[2:4, :, :, plane_lanes(p)] = slab(p, here, 1)[...] + got[2] + got[5]
-
-        def spread(step, carry, p=p):
-            cross_plane(p, step).start()
-            return carry
-
-        lax.fori_loop(1, 16, spread, 0)
+        spread(lambda di, dj, p=p: cross_plane(p, di, dj))
 
     pass_on(3)
     for q in range(3):
         total_side(q).wait_recv()
     total_plane_ref[...] = total_half_ref[3] + total_side_ref[0] + total_side_ref[1] + total_side_ref[2]
 
-    def total_plane(step):
-        i, j = (x + step // 4) % 4, (z + step % 4) % 4
-        return remote(
+    def total_plane(di, dj):
+        i, j = lax.rem(x + di, 4), lax.rem(z + dj, 4)
+        remote(
             total_plane_ref.at[:, i, j],
-            total_got_ref.at[step],
+            total_got_ref.at[di * 4 + dj],
             total_plane_send,
             total_plane_recv,
             device(x=i, z=j),
-        )
-
-    def spread_total(step, carry):
-        total_plane(step).start()
-        return carry
-
-    lax.fori_loop(1, 16, spread_total, 0)
-
+        ).start()
+
+    spread(total_plane)
     for p in range(3):
         axes = PARTS[p][3]
         drain(cross_got_ref.at[pl.ds(1, 15), :, plane_lanes(p)], cross_plane_recv.at[p])
         acc = cross_plane_ref[at[axes[0]], at[axes[1]], :, plane_lanes(p)]
         for step in range(1, 16):
             acc = acc + cross_got_ref[step, :, plane_lanes(p)]
-        out_cross_ref[:, plane_lanes(p)] = acc / jnp.sqrt(jnp.float32(NEAR * DEVICES))
+        out_cross_ref[:, plane_lanes(p)] = acc
     drain(total_got_ref.at[pl.ds(1, 15)], total_plane_recv)
-    spread_counts = jnp.broadcast_to(counted, (8, 128))
     for half in range(2):
         acc = total_plane_ref[half, x, z]
         for step in range(1, 16):
             acc = acc + total_got_ref[step, half]
-        where = (half * 8 + iota((8, 128), 1) // DS) * 8 + iota((8, 128), 0)
-        mean = acc / (jnp.take_along_axis(spread_counts, where, axis=1) + 1.0)
-        for j in range(8):
-            out_book_ref[half * 8 + j] = mean[:, j * DS : (j + 1) * DS]
+        out_total_ref[half] = acc
+    out_counts_ref[...] = jnp.broadcast_to(counted, (8, 128))
 
     drain(message_ref.at[pl.ds(0, DEVICES - 1)], message_send)
 
@@ -533,27 +560,40 @@
     drain(total_got_ref.at[pl.ds(1, 15)], total_plane_send)
 
 
+def finish_kernel(total_ref, counts_ref, cross_ref, out_book_ref, out_cross_ref):
+    out_cross_ref[...] = cross_ref[...] / jnp.sqrt(jnp.float32(NEAR * DEVICES))
+    for half in range(2):
+        where = (half * 8 + (iota((8, 128), 1) >> 4)) * 8 + iota((8, 128), 0)
+        counts = jnp.take_along_axis(counts_ref[...], where, axis=1)
+        mean = total_ref[half] / (counts + 1.0)
+        for j in range(8):
+            out_book_ref[half * 8 + j] = mean[:, j * DS : (j + 1) * DS]
+
+
 def per_device(vectors, coarse_list, list_slot, codes, centroids, rotation, codebook):
-    slot_of = list_slot[coarse_list].reshape(1, NEAR)
     book = codebook.transpose(0, 2, 1).reshape(D, K)
     here = pl.BlockSpec(memory_space=VMEM)
     away = pl.BlockSpec(memory_space=ANY)
-    return pl.pallas_call(
+    total, counts, cross = pl.pallas_call(
         kernel,
-        out_shape=(jax.ShapeDtypeStruct((16, 8, DS), F32), jax.ShapeDtypeStruct((8, D), F32)),
-        in_specs=[here, here, here, away, away, away],
-        out_specs=(here, here),
+        out_shape=(
+            jax.ShapeDtypeStruct((2, 8, 128), F32),
+            jax.ShapeDtypeStruct((8, 128), F32),
+            jax.ShapeDtypeStruct((8, D), F32),
+        ),
+        in_specs=[pl.BlockSpec(memory_space=pltpu.SMEM), here, here, here, away, away, away, away],
+        out_specs=(here, here, here),
         scratch_shapes=[
+            VMEM((LISTS, 128), I32),
+            VMEM((NEAR, 128), I32),
             VMEM((NEAR, D), BF),
             VMEM((D, D), BF),
             VMEM((2, CHUNK, D), BF),
             VMEM((LISTS * 8 + 64, 128), F32),
-            VMEM((NEAR, 128), F32),
             VMEM((D, K), F32),
             VMEM((DEVICES, SLOT, 128), BF),
             VMEM((DEVICES, SLOT, 128), BF),
             VMEM((DEVICES * SLOT, 128), F32),
-            VMEM((M, NEAR), I32),
             VMEM((M, FAR), I32),
             VMEM((16, 128), I32),
             pltpu.SMEM((16, 128), I32),
@@ -573,7 +613,7 @@
             VMEM((3, 2, 4, 4, 8, 128), F32),
             VMEM((2, 4, 4, 8, 128), F32),
             VMEM((16, 2, 8, 128), F32),
-            DMA((3,)),
+            DMA((4,)),
             DMA((2,)),
             DMA,
             DMA,
@@ -594,7 +634,23 @@
             collective_id=0, has_side_effects=True, vmem_limit_bytes=56 * 2**20
         ),
         name="refine",
-    )(slot_of, codes, book, vectors, rotation, centroids)
+    )(
+        coarse_list,
+        coarse_list.reshape(1, NEAR),
+        codes.T,
+        book,
+        list_slot.reshape(LISTS, 128),
+        vectors,
+        rotation,
+        centroids,
+    )
+    return pl.pallas_call(
+        finish_kernel,
+        out_shape=(jax.ShapeDtypeStruct((16, 8, DS), F32), jax.ShapeDtypeStruct((8, D), F32)),
+        in_specs=[here] * 3,
+        out_specs=(here, here),
+        name="finish",
+    )(total, counts, cross)
 
 
 def solution(mesh):

time: 84.7 us -> 69.9 us (0.83)
  local copies, waits for them, and re-layouts: 7.5 us -> 0 us
  Pallas kernels: 75.3 us -> 69 us
    pallas_call x1 -> x2, Pallas kernels: 75.3 us -> 69 us  [the longest x1 67.4 us: per_device(): pl.pallas_call(kernel, out_shape=(jax.ShapeDtypeStruct((2, 8, 128), F32),...]
    unnamed x5 -> x0, local copies, waits for them, and re-layouts: 5.19 us -> none
    gather x1 -> x0, local copies, waits for them, and re-layouts: 2.31 us -> none  [per_device(): slot_of = list_slot[coarse_list].reshape(1, NEAR)]
where the time goes in v3:
time: 69.9 us; the launch traced here: 69.6 us
  Pallas kernels  69 us (99%)
    pallas_call x1, Pallas kernels, per_device(): pl.pallas_call(kernel, out_shape=(jax.ShapeDtypeStruct((2, 8, 128), F32),...  67.4 us
    pallas_call x1, Pallas kernels, per_device(): pl.pallas_call(finish_kernel, out_shape=(jax.ShapeDtypeStruct((16, 8, DS)...  1.58 us

profile of v3, /device:TPU:0, one launch (start us, length us, event | category | flops | bytes accessed | tf_op | source)
XLA Modules:
  0.0 69.6 jit_solution(12998335203637740112)
XLA Ops:
  0.6 67.4 %refine.1 = (f32[2,8,128]{2,1,0:T(8,128)}, f32[8,128]{1,0:T(8,128)}, f32[8,1024]{1,0:T(8,128)}) custom-call(s32[256]{0:T(256)} %coarse_smem.1, s32[1,256]{1,0:T(1,128)} %bitcast.9, s32[64,256]{1,0:T(8,128)} %bitcast.8, bf16[1024,256]{1,0:T(8,128)(2,1)} %bitcast.7, s32[4096,128]{1,0:T(8,128)} %bitcast.6, bf16[256,1024]{1,0:T(8,128)(2,1)} %vectors_hbm.1, ...), custom_call_target="tpu_custom_call" | custom-call | tf_op jit(solution)/shard_map/refine/pallas_call | solution.py:577
  68.0 1.6 %finish.1 = (f32[16,8,16]{2,1,0:T(8,128)}, f32[8,1024]{1,0:T(8,128)}) custom-call(f32[2,8,128]{2,1,0:T(8,128)} %get-tuple-element.5.total_ref, f32[8,128]{1,0:T(8,128)} %get-tuple-element.6.counts_ref, f32[8,1024]{1,0:T(8,128)} %get-tuple-element.7.cross_ref), custom_call_target="tpu_custom_call" | custom-call | tf_op jit(solution)/shard_map/finish/pallas_call | solution.py:647

commit v4 on v3

--- a/solution.py
+++ b/solution.py
@@ -25,7 +25,6 @@
 DMA = pltpu.SemaphoreType.DMA
 
 PARTS = ((0, 384, "x", "zy"), (384, 768, "y", "xz"), (768, 1024, "z", "xy"))
-DIMS = "xzy"
 NT = (((1,), (1,)), ((), ()))
 TT = (((0,), (1,)), ((), ()))
 
@@ -69,6 +68,7 @@
     arrived_ref,
     arrived_wide_ref,
     far_codes_ref,
+    far_blocks_ref,
     row_ref,
     row_smem,
     counts_ref,
@@ -80,7 +80,9 @@
     cross_ref,
     total_ref,
     cross_half_ref,
-    ring_refs,
+    over_x_ref,
+    over_y_ref,
+    over_z_ref,
     cross_plane_ref,
     cross_got_ref,
     total_half_ref,
@@ -93,8 +95,12 @@
     message_recv,
     cross_core_send,
     cross_core_recv,
-    ring_send,
-    ring_recv,
+    over_x_send,
+    over_x_recv,
+    over_y_send,
+    over_y_recv,
+    over_z_send,
+    over_z_recv,
     cross_plane_send,
     cross_plane_recv,
     total_core_send,
@@ -136,28 +142,33 @@
     ]
     slots_load = pltpu.make_async_copy(slots_hbm, slots_ref, local_sem.at[3])
     slots_load.start()
-    greet(0, 1)
 
     level32, level128 = levels(32, NEAR), levels(128, NEAR)
     counts_ref[...] = jnp.zeros((128, 128), F32)
 
     def count(i):
         acc = jnp.zeros((32, 128), F32)
-        for j in range(2):
-            m = i * 2 + j
+        for j in range(8):
+            m = i * 8 + j
             row = near_codes_ref[pl.ds(m, 1), :]
             upper = onehot((row >> 3).astype(F32).astype(BF), level32)
             lower = onehot(((row & 7) + 8 * lax.rem(m, 16)).astype(F32).astype(BF), level128)
             acc = acc + lax.dot_general(upper, lower, NT, preferred_element_type=F32)
-        counts_ref[pl.ds(pl.multiple_of(lax.div(i, 8) * 32, 32), 32), :] += acc
-
-    def greet_and_count(dr, carry):
-        greet(dr, 0)
-        count(dr)
-        return carry
-
-    lax.fori_loop(1, 32, greet_and_count, 0)
-    count(0)
+        counts_ref[pl.ds(pl.multiple_of(lax.div(i, 2) * 32, 32), 32), :] += acc
+
+    def greet_and_count(i, carry):
+        for k in range(4):
+            greet(i * 4 + k, 0)
+        count(i)
+        return carry
+
+    for k in range(4):
+        greet(k, 1 if k == 0 else 0)
+    count(jnp.int32(0))
+    lax.fori_loop(1, 8, greet_and_count, 0)
+    for i in range(8):
+        rows = pl.ds(i * 128, 128)
+        table_book_ref[rows, :] = book_ref[rows, :].astype(F32)
 
     slots_load.wait()
     for load in loads:
@@ -213,40 +224,37 @@
                 message_ref.at[other[0] * 4 + other[1]], arrived_ref.at[me], message_send, message_recv, other
             ).start()
 
-    post(0, 1)
-
-    def post_row(dr, carry):
-        post(dr, 0)
-        return carry
-
-    lax.fori_loop(1, DEVICES // 4, post_row, 0)
+    def decode(codes, target, i, span):
+        for j in range(8):
+            m = i * 8 + j
+            index = jnp.broadcast_to(codes(m), (8, 128))
+            low, high = index & 127, index >= 128
+            halves = []
+            for half in range(2):
+                start = pl.multiple_of(m * DS + 8 * half, 8)
+                first = jnp.take_along_axis(table_book_ref[pl.ds(start, 8), 0:128], low, axis=1)
+                second = jnp.take_along_axis(table_book_ref[pl.ds(start, 8), 128:256], low, axis=1)
+                halves.append(jnp.where(high, second, first))
+            target[pl.ds(pl.multiple_of(m * DS, DS), DS), span] = jnp.concatenate(halves, 0).astype(BF)
+
+    def near_decode(i):
+        for block in range(NEAR // 128):
+            span = slice(block * 128, (block + 1) * 128)
+            decode(lambda m, span=span: near_codes_ref[pl.ds(m, 1), :][:, span], near_reb_ref, i, span)
+
+    def post_and_decode(i, carry):
+        for k in range(4):
+            post(i * 4 + k, 0)
+        near_decode(i)
+        return carry
+
+    for k in range(4):
+        post(k, 1 if k == 0 else 0)
+    lax.fori_loop(1, 8, post_and_decode, 0)
+    near_decode(jnp.int32(0))
     arrived_ref[me] = message_ref[me]
 
-    for i in range(8):
-        rows = pl.ds(i * 128, 128)
-        table_book_ref[rows, :] = book_ref[rows, :].astype(F32)
-
-    def decode(codes, target, width):
-        def step(i, carry):
-            for j in range(8):
-                m = i * 8 + j
-                row = codes[pl.ds(m, 1), :]
-                for block in range(width // 128):
-                    span = slice(block * 128, (block + 1) * 128)
-                    index = jnp.broadcast_to(row[:, span], (8, 128))
-                    low, high = index & 127, index >= 128
-                    halves = []
-                    for half in range(2):
-                        start = pl.multiple_of(m * DS + 8 * half, 8)
-                        first = jnp.take_along_axis(table_book_ref[pl.ds(start, 8), 0:128], low, axis=1)
-                        second = jnp.take_along_axis(table_book_ref[pl.ds(start, 8), 128:256], low, axis=1)
-                        halves.append(jnp.where(high, second, first))
-                    target[pl.ds(pl.multiple_of(m * DS, DS), DS), span] = jnp.concatenate(halves, 0).astype(BF)
-            return carry
-
-        lax.fori_loop(0, M // 8, step, 0)
-
-    def rotate(source, width):
+    def rotate(source, width, begin, end):
         def step(i, carry):
             columns = pl.ds(pl.multiple_of(i * 256, 256), 256)
             turned = lax.dot_general(rotation_ref[:, columns], source[...], TT, preferred_element_type=F32)
@@ -256,7 +264,7 @@
             turned_ref[pl.ds(i * 16, 16), DS : 2 * DS, 0:width] = lower.reshape(16, DS, width)
             return carry
 
-        lax.fori_loop(0, 4, step, 0)
+        lax.fori_loop(begin, end, step, 0)
 
     def group(codes, g, width):
         level = levels(128, width)
@@ -278,7 +286,6 @@
 
     loads[0].wait()
     loads[1].wait()
-    decode(near_codes_ref, near_reb_ref, NEAR)
 
     def near_cross(i, carry):
         columns = pl.ds(pl.multiple_of(i * 256, 256), 256)
@@ -287,7 +294,7 @@
         return carry
 
     lax.fori_loop(0, 4, near_cross, 0)
-    rotate(vectors_ref, NEAR)
+    rotate(vectors_ref, NEAR, 0, 4)
 
     def near_total(g, carry):
         lower, upper = group(near_codes_ref, g, NEAR)
@@ -326,6 +333,7 @@
     for j in range(CAP):
         turned_over = arrived_wide_ref[pl.ds(j, DEVICES, stride=SLOT), :].T.astype(I32) - 1
         far_codes_ref[:, j * 128 : (j + 1) * 128] = turned_over[0:M]
+        far_blocks_ref[j] = turned_over[0:M]
         upper, lower = turned_over[M : M + 1], turned_over[M + 1 : M + 2]
         row = jnp.clip(jnp.where(upper < 0, LISTS, upper * 64 + lower), 0, LISTS)
         row_ref[j : j + 1, :] = (row >> 3) * 64 + (row & 7)
@@ -334,7 +342,6 @@
     counted = jnp.sum(arrived_wide_ref[pl.ds(CAP, DEVICES, stride=SLOT), :], axis=0, keepdims=True)
     fetch = pltpu.make_async_copy(row_ref, row_smem, local_sem.at[2])
     fetch.start()
-    decode(far_codes_ref, far_reb_ref, FAR)
     fetch.wait()
 
     def gather(j, carry):
@@ -342,6 +349,8 @@
             pieces = [table_ref[pl.ds(row_smem[j, k * 16 + s], 8, stride=8), :] for s in range(16)]
             for s in range(16):
                 stage_ref[pl.ds(k * 128 + (s // 8) * 64 + s % 8, 8, stride=8), :] = pieces[s]
+            span = pl.ds(pl.multiple_of(j * 128, 128), 128)
+            decode(lambda m: far_blocks_ref[j, pl.ds(m, 1), :], far_reb_ref, k, span)
             return inner
 
         lax.fori_loop(0, 8, take, 0)
@@ -354,71 +363,72 @@
 
     lax.fori_loop(0, CAP, gather, 0)
 
-    def cross_core(i):
+    def slab(q):
+        return lax.rem(x + 1 + q, 4)
+
+    def cross_core(q):
         return remote(
-            cross_ref.at[i, :, 1 - core],
-            cross_half_ref.at[i],
-            cross_core_send.at[i],
-            cross_core_recv.at[i],
+            cross_ref.at[slab(q), :, 1 - core],
+            cross_half_ref.at[slab(q)],
+            cross_core_send.at[q],
+            cross_core_recv.at[q],
             mate,
         )
 
-    def far_cross(i, carry):
+    def lanes(p):
+        return slice(PARTS[p][0], PARTS[p][1])
+
+    def over_x(q):
+        i = slab(q)
+        return remote(
+            cross_half_ref.at[i, :, :, :, lanes(0)], over_x_ref.at[q], over_x_send.at[q], over_x_recv.at[q], device(x=i)
+        )
+
+    def over_y(q, s):
+        i, j = slab(q), lax.rem(y + s, 4)
+        return remote(
+            cross_half_ref.at[i, :, j, :, lanes(1)],
+            over_y_ref.at[s - 1, i],
+            over_y_send.at[q, s - 1],
+            over_y_recv.at[q, s - 1],
+            device(y=j),
+        )
+
+    def over_z(q, s):
+        i, j = slab(q), lax.rem(z + s, 4)
+        return remote(
+            cross_half_ref.at[i, j, :, :, lanes(2)],
+            over_z_ref.at[s - 1, i],
+            over_z_send.at[q, s - 1],
+            over_z_recv.at[q, s - 1],
+            device(z=j),
+        )
+
+    def join(q):
+        cross_core(q).wait_recv()
+        cross_half_ref[slab(q)] += cross_ref[slab(q), :, core]
+        for s in range(1, 4):
+            over_y(q, s).start()
+            over_z(q, s).start()
+
+    def far_cross(q, carry):
+        i = slab(q)
         columns = pl.ds(pl.multiple_of(i * 256, 256), 256)
         block = lax.dot_general(far_x_ref[:, columns], far_reb_ref[...], TT, preferred_element_type=F32)
         cross_ref[i] += block.reshape(4, 2, 4, 8, D)
-        cross_core(i).start()
+        cross_core(q).start()
+
+        @pl.when(q >= 1)
+        def _():
+            join(q - 1)
+            over_x(q - 1).start()
+
         return carry
 
     lax.fori_loop(0, 4, far_cross, 0)
-    rotate(far_x_ref, FAR)
-
-    def join(i, carry):
-        cross_core(i).wait_recv()
-        cross_half_ref[i] += cross_ref[i, :, core]
-        return carry
-
-    lax.fori_loop(0, 4, join, 0)
-
-    def slab(p, value, half):
-        begin, end, axis, _ = PARTS[p]
-        rest = [d for d in DIMS if d != axis]
-        index = []
-        for d in DIMS:
-            if d == axis:
-                index.append(value)
-            elif d == rest[0]:
-                index.append(pl.ds(half * 2, 2))
-            else:
-                index.append(slice(None))
-        return cross_half_ref.at[tuple(index) + (slice(None), slice(begin, end))]
-
-    def ring(p, slot, value, half, way):
-        axis = PARTS[p][2]
-        return remote(
-            slab(p, value, half),
-            ring_refs[p].at[slot],
-            ring_send.at[p, slot],
-            ring_recv.at[p, slot],
-            device(**{axis: lax.rem(at[axis] + way, 4)}),
-        )
-
-    def around(p):
-        here = at[PARTS[p][2]]
-        return here, lax.rem(here + 1, 4), lax.rem(here + 2, 4), lax.rem(here + 3, 4)
-
-    first, second = [], []
-    for p in range(3):
-        here, after, beyond, before = around(p)
-        copies = [
-            ring(p, 0, beyond, 0, 1),
-            ring(p, 1, beyond, 1, 3),
-            ring(p, 2, after, 1, 1),
-            ring(p, 3, before, 0, 3),
-        ]
-        for copy in copies:
-            copy.start()
-        first.append(copies)
+    rotate(far_x_ref, FAR, 0, 2)
+    join(3)
+    rotate(far_x_ref, FAR, 2, 4)
 
     def side(q):
         return lax.rem(y + 1 + q, 4)
@@ -457,29 +467,6 @@
         if q < 3:
             total_side(q).start()
 
-    far_total(0)
-    far_total(1)
-    pass_on(0)
-    for p in range(3):
-        here, after, beyond, before = around(p)
-        first[p][0].wait_recv()
-        target = slab(p, after, 0)
-        target[...] += ring_refs[p][0]
-        first[p][1].wait_recv()
-        target = slab(p, before, 1)
-        target[...] += ring_refs[p][1]
-        copies = [ring(p, 4, after, 0, 1), ring(p, 5, before, 1, 3)]
-        for copy in copies:
-            copy.start()
-        second.append(copies)
-    far_total(2)
-    pass_on(1)
-    far_total(3)
-    pass_on(2)
-
-    def plane_lanes(p):
-        return slice(PARTS[p][0], PARTS[p][1])
-
     def spread(start):
         for j in range(1, 4):
             start(0, j)
@@ -495,22 +482,43 @@
         axes = PARTS[p][3]
         i, j = lax.rem(at[axes[0]] + di, 4), lax.rem(at[axes[1]] + dj, 4)
         remote(
-            cross_plane_ref.at[i, j, :, plane_lanes(p)],
-            cross_got_ref.at[di * 4 + dj, :, plane_lanes(p)],
+            cross_plane_ref.at[i, j, :, lanes(p)],
+            cross_got_ref.at[di * 4 + dj, :, lanes(p)],
             cross_plane_send.at[p],
             cross_plane_recv.at[p],
             device(**{axes[0]: i, axes[1]: j}),
         ).start()
 
-    for p in range(3):
-        here = around(p)[0]
-        for copy in first[p][2:] + second[p]:
-            copy.wait_recv()
-        got = ring_refs[p]
-        cross_plane_ref[0:2, :, :, plane_lanes(p)] = slab(p, here, 0)[...] + got[3] + got[4]
-        cross_plane_ref[2:4, :, :, plane_lanes(p)] = slab(p, here, 1)[...] + got[2] + got[5]
-        spread(lambda di, dj, p=p: cross_plane(p, di, dj))
-
+    far_total(0)
+    far_total(1)
+    pass_on(0)
+    far_total(2)
+    pass_on(1)
+
+    for q in range(3):
+        over_x(q).wait_recv()
+    cross_plane_ref[:, :, :, lanes(0)] = (
+        cross_half_ref[x, :, :, :, lanes(0)] + over_x_ref[0] + over_x_ref[1] + over_x_ref[2]
+    )
+    spread(lambda di, dj: cross_plane(0, di, dj))
+
+    def arrived_over(q, carry):
+        for s in range(1, 4):
+            over_y(q, s).wait_recv()
+            over_z(q, s).wait_recv()
+        return carry
+
+    lax.fori_loop(0, 4, arrived_over, 0)
+    cross_plane_ref[:, :, :, lanes(1)] = (
+        cross_half_ref[:, :, y, :, lanes(1)] + over_y_ref[0] + over_y_ref[1] + over_y_ref[2]
+    )
+    spread(lambda di, dj: cross_plane(1, di, dj))
+    cross_plane_ref[:, :, :, lanes(2)] = (
+        cross_half_ref[:, z, :, :, lanes(2)] + over_z_ref[0] + over_z_ref[1] + over_z_ref[2]
+    )
+    spread(lambda di, dj: cross_plane(2, di, dj))
+    far_total(3)
+    pass_on(2)
     pass_on(3)
     for q in range(3):
         total_side(q).wait_recv()
@@ -529,11 +537,11 @@
     spread(total_plane)
     for p in range(3):
         axes = PARTS[p][3]
-        drain(cross_got_ref.at[pl.ds(1, 15), :, plane_lanes(p)], cross_plane_recv.at[p])
-        acc = cross_plane_ref[at[axes[0]], at[axes[1]], :, plane_lanes(p)]
+        drain(cross_got_ref.at[pl.ds(1, 15), :, lanes(p)], cross_plane_recv.at[p])
+        acc = cross_plane_ref[at[axes[0]], at[axes[1]], :, lanes(p)]
         for step in range(1, 16):
-            acc = acc + cross_got_ref[step, :, plane_lanes(p)]
-        out_cross_ref[:, plane_lanes(p)] = acc
+            acc = acc + cross_got_ref[step, :, lanes(p)]
+        out_cross_ref[:, lanes(p)] = acc
     drain(total_got_ref.at[pl.ds(1, 15)], total_plane_recv)
     for half in range(2):
         acc = total_plane_ref[half, x, z]
@@ -544,15 +552,17 @@
 
     drain(message_ref.at[pl.ds(0, DEVICES - 1)], message_send)
 
-    def left(i, carry):
-        cross_core(i).wait_send()
+    def left(q, carry):
+        cross_core(q).wait_send()
+        for s in range(1, 4):
+            over_y(q, s).wait_send()
+            over_z(q, s).wait_send()
         return carry
 
     lax.fori_loop(0, 4, left, 0)
     for p in range(3):
-        for copy in first[p] + second[p]:
-            copy.wait_send()
-        drain(cross_got_ref.at[pl.ds(1, 15), :, plane_lanes(p)], cross_plane_send.at[p])
+        over_x(p).wait_send()
+        drain(cross_got_ref.at[pl.ds(1, 15), :, lanes(p)], cross_plane_send.at[p])
     for q in range(4):
         total_core(q).wait_send()
         if q < 3:
@@ -595,6 +605,7 @@
             VMEM((DEVICES, SLOT, 128), BF),
             VMEM((DEVICES * SLOT, 128), F32),
             VMEM((M, FAR), I32),
+            VMEM((CAP, M, 128), I32),
             VMEM((16, 128), I32),
             pltpu.SMEM((16, 128), I32),
             VMEM((128, 128), F32),
@@ -606,7 +617,9 @@
             VMEM((4, 4, 2, 4, 8, D), F32),
             VMEM((2, 4, 4, 2, 4, 8, 128), F32),
             VMEM((4, 4, 4, 8, D), F32),
-            [VMEM((6, 2, 4, 8, end - begin), F32) for begin, end, _, _ in PARTS],
+            VMEM((3, 4, 4, 8, 384), F32),
+            VMEM((3, 4, 4, 8, 384), F32),
+            VMEM((3, 4, 4, 8, 256), F32),
             VMEM((4, 4, 8, D), F32),
             VMEM((16, 8, D), F32),
             VMEM((4, 2, 4, 4, 8, 128), F32),
@@ -619,8 +632,12 @@
             DMA,
             DMA((4,)),
             DMA((4,)),
-            DMA((3, 6)),
-            DMA((3, 6)),
+            DMA((3,)),
+            DMA((3,)),
+            DMA((4, 3)),
+            DMA((4, 3)),
+            DMA((4, 3)),
+            DMA((4, 3)),
             DMA((3,)),
             DMA((3,)),
             DMA((4,)),

time: 69.9 us -> 73.2 us (1.047)
  Pallas kernels: 69 us -> 72.3 us
    pallas_call x1, Pallas kernels: 67.4 us -> 70.7 us  [per_device(): pl.pallas_call(kernel, out_shape=(jax.ShapeDtypeStruct((2, 8, 128), F32),...]
where the time goes in v4:
time: 73.2 us; the launch traced here: 72.9 us
  Pallas kernels  72.3 us (99%)
    pallas_call x1, Pallas kernels, per_device(): pl.pallas_call(kernel, out_shape=(jax.ShapeDtypeStruct((2, 8, 128), F32),...  70.7 us
    pallas_call x1, Pallas kernels, per_device(): pl.pallas_call(finish_kernel, out_shape=(jax.ShapeDtypeStruct((16, 8, DS)...  1.58 us

profile of v4, /device:TPU:0, one launch (start us, length us, event | category | flops | bytes accessed | tf_op | source)
XLA Modules:
  0.0 72.9 jit_solution(1244957296551445676)
XLA Ops:
  0.6 70.7 %refine.1 = (f32[2,8,128]{2,1,0:T(8,128)}, f32[8,128]{1,0:T(8,128)}, f32[8,1024]{1,0:T(8,128)}) custom-call(s32[256]{0:T(256)} %coarse_smem.1, s32[1,256]{1,0:T(1,128)} %bitcast.9, s32[64,256]{1,0:T(8,128)} %bitcast.8, bf16[1024,256]{1,0:T(8,128)(2,1)} %bitcast.7, s32[4096,128]{1,0:T(8,128)} %bitcast.6, bf16[256,1024]{1,0:T(8,128)(2,1)} %vectors_hbm.1, ...), custom_call_target="tpu_custom_call" | custom-call | tf_op jit(solution)/shard_map/refine/pallas_call | solution.py:587
  71.4 1.6 %finish.1 = (f32[16,8,16]{2,1,0:T(8,128)}, f32[8,1024]{1,0:T(8,128)}) custom-call(f32[2,8,128]{2,1,0:T(8,128)} %get-tuple-element.5.total_ref, f32[8,128]{1,0:T(8,128)} %get-tuple-element.6.counts_ref, f32[8,1024]{1,0:T(8,128)} %get-tuple-element.7.cross_ref), custom_call_target="tpu_custom_call" | custom-call | tf_op jit(solution)/shard_map/finish/pallas_call | solution.py:664

commit v5 on v4

--- a/solution.py
+++ b/solution.py
@@ -24,7 +24,7 @@
 ANY = pl.ANY
 DMA = pltpu.SemaphoreType.DMA
 
-PARTS = ((0, 384, "x", "zy"), (384, 768, "y", "xz"), (768, 1024, "z", "xy"))
+PARTS = ((0, 384, "x", "zy"), (384, 640, "y", "xz"), (640, 1024, "z", "xy"))
 NT = (((1,), (1,)), ((), ()))
 TT = (((0,), (1,)), ((), ()))
 
@@ -68,7 +68,6 @@
     arrived_ref,
     arrived_wide_ref,
     far_codes_ref,
-    far_blocks_ref,
     row_ref,
     row_smem,
     counts_ref,
@@ -333,7 +332,6 @@
     for j in range(CAP):
         turned_over = arrived_wide_ref[pl.ds(j, DEVICES, stride=SLOT), :].T.astype(I32) - 1
         far_codes_ref[:, j * 128 : (j + 1) * 128] = turned_over[0:M]
-        far_blocks_ref[j] = turned_over[0:M]
         upper, lower = turned_over[M : M + 1], turned_over[M + 1 : M + 2]
         row = jnp.clip(jnp.where(upper < 0, LISTS, upper * 64 + lower), 0, LISTS)
         row_ref[j : j + 1, :] = (row >> 3) * 64 + (row & 7)
@@ -342,6 +340,14 @@
     counted = jnp.sum(arrived_wide_ref[pl.ds(CAP, DEVICES, stride=SLOT), :], axis=0, keepdims=True)
     fetch = pltpu.make_async_copy(row_ref, row_smem, local_sem.at[2])
     fetch.start()
+
+    def far_decode(i, carry):
+        for block in range(CAP):
+            span = slice(block * 128, (block + 1) * 128)
+            decode(lambda m, span=span: far_codes_ref[pl.ds(m, 1), :][:, span], far_reb_ref, i, span)
+        return carry
+
+    lax.fori_loop(0, M // 8, far_decode, 0)
     fetch.wait()
 
     def gather(j, carry):
@@ -349,8 +355,6 @@
             pieces = [table_ref[pl.ds(row_smem[j, k * 16 + s], 8, stride=8), :] for s in range(16)]
             for s in range(16):
                 stage_ref[pl.ds(k * 128 + (s // 8) * 64 + s % 8, 8, stride=8), :] = pieces[s]
-            span = pl.ds(pl.multiple_of(j * 128, 128), 128)
-            decode(lambda m: far_blocks_ref[j, pl.ds(m, 1), :], far_reb_ref, k, span)
             return inner
 
         lax.fori_loop(0, 8, take, 0)
@@ -418,27 +422,30 @@
         cross_ref[i] += block.reshape(4, 2, 4, 8, D)
         cross_core(q).start()
 
-        @pl.when(q >= 1)
+        @pl.when(q >= 2)
         def _():
-            join(q - 1)
-            over_x(q - 1).start()
+            join(q - 2)
+            over_x(q - 2).start()
 
         return carry
 
     lax.fori_loop(0, 4, far_cross, 0)
-    rotate(far_x_ref, FAR, 0, 2)
+    rotate(far_x_ref, FAR, 0, 1)
+    join(2)
+    over_x(2).start()
+    rotate(far_x_ref, FAR, 1, 2)
     join(3)
     rotate(far_x_ref, FAR, 2, 4)
 
     def side(q):
         return lax.rem(y + 1 + q, 4)
 
-    def total_core(q):
+    def total_core(q, half):
         return remote(
-            total_ref.at[:, :, :, 1 - core, side(q)],
-            total_half_ref.at[q],
-            total_core_send.at[q],
-            total_core_recv.at[q],
+            total_ref.at[half, :, :, 1 - core, side(q)],
+            total_half_ref.at[q, half],
+            total_core_send.at[q, half],
+            total_core_recv.at[q, half],
             mate,
         )
 
@@ -451,21 +458,22 @@
             (r, side(q)),
         )
 
-    def far_total(q):
+    def far_total(q, begin, end):
         def step(half, carry):
             lower, upper = group(far_codes_ref, side(q) * 2 + half, FAR)
             total_ref[half, 0:2, :, :, side(q)] += lower.reshape(2, 4, 2, 8, 128)
             total_ref[half, 2:4, :, :, side(q)] += upper.reshape(2, 4, 2, 8, 128)
+            total_core(q, half).start(0)
             return carry
 
-        lax.fori_loop(0, 2, step, 0)
-        total_core(q).start()
+        lax.fori_loop(begin, end, step, 0)
 
     def pass_on(q):
-        total_core(q).wait_recv()
+        for half in range(2):
+            total_core(q, half).wait_recv()
         total_half_ref[q] += total_ref[:, :, :, core, side(q)]
         if q < 3:
-            total_side(q).start()
+            total_side(q).start(0)
 
     def spread(start):
         for j in range(1, 4):
@@ -489,12 +497,17 @@
             device(**{axes[0]: i, axes[1]: j}),
         ).start()
 
-    far_total(0)
-    far_total(1)
+    far_total(0, 0, 2)
+    far_total(1, 0, 1)
     pass_on(0)
-    far_total(2)
+    far_total(1, 1, 2)
+    far_total(2, 0, 1)
     pass_on(1)
-
+    far_total(2, 1, 2)
+
+    far_total(3, 0, 1)
+    pass_on(2)
+    far_total(3, 1, 2)
     for q in range(3):
         over_x(q).wait_recv()
     cross_plane_ref[:, :, :, lanes(0)] = (
@@ -517,8 +530,6 @@
         cross_half_ref[:, z, :, :, lanes(2)] + over_z_ref[0] + over_z_ref[1] + over_z_ref[2]
     )
     spread(lambda di, dj: cross_plane(2, di, dj))
-    far_total(3)
-    pass_on(2)
     pass_on(3)
     for q in range(3):
         total_side(q).wait_recv()
@@ -532,7 +543,7 @@
             total_plane_send,
             total_plane_recv,
             device(x=i, z=j),
-        ).start()
+        ).start(0)
 
     spread(total_plane)
     for p in range(3):
@@ -564,7 +575,8 @@
         over_x(p).wait_send()
         drain(cross_got_ref.at[pl.ds(1, 15), :, lanes(p)], cross_plane_send.at[p])
     for q in range(4):
-        total_core(q).wait_send()
+        for half in range(2):
+            total_core(q, half).wait_send()
         if q < 3:
             total_side(q).wait_send()
     drain(total_got_ref.at[pl.ds(1, 15)], total_plane_send)
@@ -605,7 +617,6 @@
             VMEM((DEVICES, SLOT, 128), BF),
             VMEM((DEVICES * SLOT, 128), F32),
             VMEM((M, FAR), I32),
-            VMEM((CAP, M, 128), I32),
             VMEM((16, 128), I32),
             pltpu.SMEM((16, 128), I32),
             VMEM((128, 128), F32),
@@ -618,8 +629,8 @@
             VMEM((2, 4, 4, 2, 4, 8, 128), F32),
             VMEM((4, 4, 4, 8, D), F32),
             VMEM((3, 4, 4, 8, 384), F32),
+            VMEM((3, 4, 4, 8, 256), F32),
             VMEM((3, 4, 4, 8, 384), F32),
-            VMEM((3, 4, 4, 8, 256), F32),
             VMEM((4, 4, 8, D), F32),
             VMEM((16, 8, D), F32),
             VMEM((4, 2, 4, 4, 8, 128), F32),
@@ -640,8 +651,8 @@
             DMA((4, 3)),
             DMA((3,)),
             DMA((3,)),
-            DMA((4,)),
-            DMA((4,)),
+            DMA((4, 2)),
+            DMA((4, 2)),
             DMA((3,)),
             DMA((3,)),
             DMA,

time: 73.2 us -> 65 us (0.89); the launches traced: 72.9 us -> 63.9 us
  Pallas kernels: 72.3 us -> 63.3 us
    pallas_call x1, Pallas kernels: 70.7 us -> 61.7 us  [per_device(): pl.pallas_call(kernel, out_shape=(jax.ShapeDtypeStruct((2, 8, 128), F32),...]
where the time goes in v5:
time: 65 us; the launch traced here: 63.9 us
  Pallas kernels  63.3 us (97%)
    pallas_call x1, Pallas kernels, per_device(): pl.pallas_call(kernel, out_shape=(jax.ShapeDtypeStruct((2, 8, 128), F32),...  61.7 us
    pallas_call x1, Pallas kernels, per_device(): pl.pallas_call(finish_kernel, out_shape=(jax.ShapeDtypeStruct((16, 8, DS)...  1.58 us

profile of v5, /device:TPU:0, one launch (start us, length us, event | category | flops | bytes accessed | tf_op | source)
XLA Modules:
  0.0 63.9 jit_solution(14981565811165609281)
XLA Ops:
  0.6 61.7 %refine.1 = (f32[2,8,128]{2,1,0:T(8,128)}, f32[8,128]{1,0:T(8,128)}, f32[8,1024]{1,0:T(8,128)}) custom-call(s32[256]{0:T(256)} %coarse_smem.1, s32[1,256]{1,0:T(1,128)} %bitcast.9, s32[64,256]{1,0:T(8,128)} %bitcast.8, bf16[1024,256]{1,0:T(8,128)(2,1)} %bitcast.7, s32[4096,128]{1,0:T(8,128)} %bitcast.6, bf16[256,1024]{1,0:T(8,128)(2,1)} %vectors_hbm.1, ...), custom_call_target="tpu_custom_call" | custom-call | tf_op jit(solution)/shard_map/refine/pallas_call | solution.py:599
  62.3 1.6 %finish.1 = (f32[16,8,16]{2,1,0:T(8,128)}, f32[8,1024]{1,0:T(8,128)}) custom-call(f32[2,8,128]{2,1,0:T(8,128)} %get-tuple-element.5.total_ref, f32[8,128]{1,0:T(8,128)} %get-tuple-element.6.counts_ref, f32[8,1024]{1,0:T(8,128)} %get-tuple-element.7.cross_ref), custom_call_target="tpu_custom_call" | custom-call | tf_op jit(solution)/shard_map/finish/pallas_call | solution.py:675

commit v6 on v5

--- a/solution.py
+++ b/solution.py
@@ -24,7 +24,9 @@
 ANY = pl.ANY
 DMA = pltpu.SemaphoreType.DMA
 
-PARTS = ((0, 384, "x", "zy"), (384, 640, "y", "xz"), (640, 1024, "z", "xy"))
+PIECES = (("y", 0, 0, 256, 0), ("x", 1, 0, 256, 0), ("z", 2, 0, 256, 0), ("x", 3, 0, 128, 256), ("z", 3, 128, 256, 256))
+WIDTH = {"x": 384, "y": 256, "z": 384}
+PLANE = {"x": "zy", "y": "xz", "z": "xy"}
 NT = (((1,), (1,)), ((), ()))
 TT = (((0,), (1,)), ((), ()))
 
@@ -79,11 +81,10 @@
     cross_ref,
     total_ref,
     cross_half_ref,
-    over_x_ref,
-    over_y_ref,
-    over_z_ref,
-    cross_plane_ref,
-    cross_got_ref,
+    over_refs,
+    near_xt_ref,
+    plane_refs,
+    got_refs,
     total_half_ref,
     total_side_ref,
     total_plane_ref,
@@ -94,12 +95,8 @@
     message_recv,
     cross_core_send,
     cross_core_recv,
-    over_x_send,
-    over_x_recv,
-    over_y_send,
-    over_y_recv,
-    over_z_send,
-    over_z_recv,
+    piece_send,
+    piece_recv,
     cross_plane_send,
     cross_plane_recv,
     total_core_send,
@@ -223,9 +220,9 @@
                 message_ref.at[other[0] * 4 + other[1]], arrived_ref.at[me], message_send, message_recv, other
             ).start()
 
-    def decode(codes, target, i, span):
-        for j in range(8):
-            m = i * 8 + j
+    def decode(codes, target, i, span, count=8):
+        for j in range(count):
+            m = i * count + j
             index = jnp.broadcast_to(codes(m), (8, 128))
             low, high = index & 127, index >= 128
             halves = []
@@ -286,10 +283,14 @@
     loads[0].wait()
     loads[1].wait()
 
-    def near_cross(i, carry):
-        columns = pl.ds(pl.multiple_of(i * 256, 256), 256)
-        block = lax.dot_general(vectors_ref[:, columns], near_reb_ref[...], TT, preferred_element_type=F32)
-        cross_ref[i] = block.reshape(4, 2, 4, 8, D)
+    for i in range(8):
+        near_xt_ref[i * 128 : (i + 1) * 128, :] = vectors_ref[:, i * 128 : (i + 1) * 128].T
+
+    def near_cross(q, carry):
+        rows = near_reb_ref[pl.ds(pl.multiple_of(q * 256, 256), 256), :]
+        for i in range(4):
+            block = lax.dot_general(near_xt_ref[i * 256 : (i + 1) * 256, :], rows, NT, preferred_element_type=F32)
+            cross_ref[q, i] = block.reshape(4, 2, 4, 8, 256)
         return carry
 
     lax.fori_loop(0, 4, near_cross, 0)
@@ -306,16 +307,18 @@
     def widen(i, carry):
         chunk_load(i).wait()
 
-        def part(k, inner):
+        def part(kk, inner):
             source = chunk_ref.at[lax.rem(i, 2)]
-            for c in range(8):
-                piece = source[pl.ds(pl.multiple_of(k * 16, 16), 16), c * 128 : (c + 1) * 128].astype(F32)
-                start = pl.multiple_of((i * (CHUNK // 16) + k) * 128 + c * 8, 8)
-                table_ref[pl.ds(start, 8), :] = piece[0:8]
-                table_ref[pl.ds(pl.multiple_of(start + 64, 8), 8), :] = piece[8:16]
+            for k in range(4):
+                for c in range(8):
+                    first = pl.multiple_of(kk * 64 + k * 16, 16)
+                    piece = source[pl.ds(first, 16), c * 128 : (c + 1) * 128].astype(F32)
+                    start = pl.multiple_of((i * (CHUNK // 64) + kk) * 512 + k * 128 + c * 8, 8)
+                    table_ref[pl.ds(start, 8), :] = piece[0:8]
+                    table_ref[pl.ds(pl.multiple_of(start + 64, 8), 8), :] = piece[8:16]
             return inner
 
-        lax.fori_loop(0, CHUNK // 16, part, 0)
+        lax.fori_loop(0, CHUNK // 64, part, 0)
 
         @pl.when(i + 2 < LISTS // CHUNK)
         def _():
@@ -341,104 +344,93 @@
     fetch = pltpu.make_async_copy(row_ref, row_smem, local_sem.at[2])
     fetch.start()
 
-    def far_decode(i, carry):
+    def far_decode(q, i):
         for block in range(CAP):
             span = slice(block * 128, (block + 1) * 128)
-            decode(lambda m, span=span: far_codes_ref[pl.ds(m, 1), :][:, span], far_reb_ref, i, span)
-        return carry
-
-    lax.fori_loop(0, M // 8, far_decode, 0)
+            decode(lambda m, span=span: far_codes_ref[pl.ds(m, 1), :][:, span], far_reb_ref, q * 4 + i, span, 4)
+
+    def first_decode(i, carry):
+        far_decode(0, i)
+        return carry
+
+    lax.fori_loop(0, 4, first_decode, 0)
     fetch.wait()
 
     def gather(j, carry):
         def take(k, inner):
-            pieces = [table_ref[pl.ds(row_smem[j, k * 16 + s], 8, stride=8), :] for s in range(16)]
-            for s in range(16):
-                stage_ref[pl.ds(k * 128 + (s // 8) * 64 + s % 8, 8, stride=8), :] = pieces[s]
+            for part in range(2):
+                pieces = [table_ref[pl.ds(row_smem[j, k * 32 + part * 16 + s], 8, stride=8), :] for s in range(16)]
+                for s in range(16):
+                    start = k * 256 + part * 128 + (s // 8) * 64 + s % 8
+                    stage_ref[pl.ds(start, 8, stride=8), :] = pieces[s]
             return inner
 
-        lax.fori_loop(0, 8, take, 0)
-        block = stage_ref[...].reshape(16, 8, 8, 128)
+        lax.fori_loop(0, 4, take, 0)
         for c in range(8):
-            far_x_ref[pl.ds(pl.multiple_of(j * 128, 128), 128), c * 128 : (c + 1) * 128] = (
-                -block[:, c].reshape(128, 128)
-            ).astype(BF)
+            for half in range(8):
+                block = [stage_ref[k * 64 + c * 8 : k * 64 + c * 8 + 8, :] for k in (half * 2, half * 2 + 1)]
+                start = pl.multiple_of(j * 128 + half * 16, 16)
+                far_x_ref[pl.ds(start, 16), c * 128 : (c + 1) * 128] = (-jnp.concatenate(block, 0)).astype(BF)
         return carry
 
     lax.fori_loop(0, CAP, gather, 0)
-
-    def slab(q):
-        return lax.rem(x + 1 + q, 4)
 
     def cross_core(q):
         return remote(
-            cross_ref.at[slab(q), :, 1 - core],
-            cross_half_ref.at[slab(q)],
+            cross_ref.at[q, :, :, 1 - core],
+            cross_half_ref.at[q],
             cross_core_send.at[q],
             cross_core_recv.at[q],
             mate,
         )
 
-    def lanes(p):
-        return slice(PARTS[p][0], PARTS[p][1])
-
-    def over_x(q):
-        i = slab(q)
+    def along_axis(axis, value):
+        return tuple(value if d == axis else slice(None) for d in "xzy")
+
+    def piece(k, step):
+        axis, q, begin, end, offset = PIECES[k]
+        there = lax.rem(at[axis] + step, 4)
         return remote(
-            cross_half_ref.at[i, :, :, :, lanes(0)], over_x_ref.at[q], over_x_send.at[q], over_x_recv.at[q], device(x=i)
-        )
-
-    def over_y(q, s):
-        i, j = slab(q), lax.rem(y + s, 4)
-        return remote(
-            cross_half_ref.at[i, :, j, :, lanes(1)],
-            over_y_ref.at[s - 1, i],
-            over_y_send.at[q, s - 1],
-            over_y_recv.at[q, s - 1],
-            device(y=j),
-        )
-
-    def over_z(q, s):
-        i, j = slab(q), lax.rem(z + s, 4)
-        return remote(
-            cross_half_ref.at[i, j, :, :, lanes(2)],
-            over_z_ref.at[s - 1, i],
-            over_z_send.at[q, s - 1],
-            over_z_recv.at[q, s - 1],
-            device(z=j),
+            cross_half_ref.at[(q,) + along_axis(axis, there) + (slice(None), slice(begin, end))],
+            over_refs[axis].at[step - 1, :, :, :, offset : offset + end - begin],
+            piece_send.at[k, step - 1],
+            piece_recv.at[k, step - 1],
+            device(**{axis: there}),
         )
 
     def join(q):
         cross_core(q).wait_recv()
-        cross_half_ref[slab(q)] += cross_ref[slab(q), :, core]
-        for s in range(1, 4):
-            over_y(q, s).start()
-            over_z(q, s).start()
-
-    def far_cross(q, carry):
-        i = slab(q)
-        columns = pl.ds(pl.multiple_of(i * 256, 256), 256)
-        block = lax.dot_general(far_x_ref[:, columns], far_reb_ref[...], TT, preferred_element_type=F32)
-        cross_ref[i] += block.reshape(4, 2, 4, 8, D)
+        cross_half_ref[q] += cross_ref[q, :, :, core]
+        for k in range(5):
+            if PIECES[k][1] == q:
+                for step in range(1, 4):
+                    piece(k, step).start()
+
+    def far_cross(q):
+        def step(i, carry):
+            columns = pl.ds(pl.multiple_of(i * 256, 256), 256)
+            rows = slice(q * 256, (q + 1) * 256)
+            block = jnp.dot(far_reb_ref[rows, :], far_x_ref[:, columns], preferred_element_type=F32)
+            if q < 3:
+                far_decode(q + 1, i)
+            cross_ref[q, i] += block.T.reshape(4, 2, 4, 8, 256)
+            return carry
+
+        lax.fori_loop(0, 4, step, 0)
+
+    for q in range(4):
+        far_cross(q)
         cross_core(q).start()
-
-        @pl.when(q >= 2)
-        def _():
+        if q >= 2:
             join(q - 2)
-            over_x(q - 2).start()
-
-        return carry
-
-    lax.fori_loop(0, 4, far_cross, 0)
     rotate(far_x_ref, FAR, 0, 1)
     join(2)
-    over_x(2).start()
     rotate(far_x_ref, FAR, 1, 2)
     join(3)
     rotate(far_x_ref, FAR, 2, 4)
 
     def side(q):
-        return lax.rem(y + 1 + q, 4)
+        return lax.rem(y + (2, 1, 3, 0)[q], 4)
 
     def total_core(q, half):
         return remote(
@@ -449,31 +441,30 @@
             mate,
         )
 
-    def total_side(q):
+    def total_side(q, half):
         return remote(
-            total_half_ref.at[q],
-            total_side_ref.at[q],
-            total_side_send.at[q],
-            total_side_recv.at[q],
+            total_half_ref.at[q, half],
+            total_side_ref.at[q, half],
+            total_side_send.at[q, half],
+            total_side_recv.at[q, half],
             (r, side(q)),
         )
 
-    def far_total(q, begin, end):
-        def step(half, carry):
-            lower, upper = group(far_codes_ref, side(q) * 2 + half, FAR)
+    def far_total(q, half):
+        def step(g, carry):
+            lower, upper = group(far_codes_ref, g, FAR)
             total_ref[half, 0:2, :, :, side(q)] += lower.reshape(2, 4, 2, 8, 128)
             total_ref[half, 2:4, :, :, side(q)] += upper.reshape(2, 4, 2, 8, 128)
-            total_core(q, half).start(0)
             return carry
 
-        lax.fori_loop(begin, end, step, 0)
-
-    def pass_on(q):
-        for half in range(2):
-            total_core(q, half).wait_recv()
-        total_half_ref[q] += total_ref[:, :, :, core, side(q)]
+        lax.fori_loop(side(q) * 2 + half, side(q) * 2 + half + 1, step, 0)
+        total_core(q, half).start()
+
+    def pass_on(q, half):
+        total_core(q, half).wait_recv()
+        total_half_ref[q, half] += total_ref[half, :, :, core, side(q)]
         if q < 3:
-            total_side(q).start(0)
+            total_side(q, half).start()
 
     def spread(start):
         for j in range(1, 4):
@@ -486,53 +477,42 @@
 
         lax.fori_loop(1, 4, row, 0)
 
-    def cross_plane(p, di, dj):
-        axes = PARTS[p][3]
+    def cross_plane(axis, di, dj):
+        axes = PLANE[axis]
         i, j = lax.rem(at[axes[0]] + di, 4), lax.rem(at[axes[1]] + dj, 4)
         remote(
-            cross_plane_ref.at[i, j, :, lanes(p)],
-            cross_got_ref.at[di * 4 + dj, :, lanes(p)],
-            cross_plane_send.at[p],
-            cross_plane_recv.at[p],
+            plane_refs[axis].at[i, j],
+            got_refs[axis].at[di * 4 + dj],
+            cross_plane_send.at["xyz".index(axis)],
+            cross_plane_recv.at["xyz".index(axis)],
             device(**{axes[0]: i, axes[1]: j}),
         ).start()
 
-    far_total(0, 0, 2)
-    far_total(1, 0, 1)
-    pass_on(0)
-    far_total(1, 1, 2)
-    far_total(2, 0, 1)
-    pass_on(1)
-    far_total(2, 1, 2)
-
-    far_total(3, 0, 1)
-    pass_on(2)
-    far_total(3, 1, 2)
+    def over(axis):
+        for k in range(5):
+            name, q, begin, end, offset = PIECES[k]
+            if name == axis:
+                for step in range(1, 4):
+                    piece(k, step).wait_recv()
+                own = cross_half_ref[(q,) + along_axis(axis, at[axis]) + (slice(None), slice(begin, end))]
+                place = slice(offset, offset + end - begin)
+                got = over_refs[axis]
+                plane_refs[axis][:, :, :, place] = (
+                    own + got[0, :, :, :, place] + got[1, :, :, :, place] + got[2, :, :, :, place]
+                )
+        spread(lambda di, dj: cross_plane(axis, di, dj))
+
+    for h in range(8):
+        far_total(h // 2, h % 2)
+        if h >= 1:
+            pass_on((h - 1) // 2, (h - 1) % 2)
+    over("y")
+    over("x")
+    over("z")
+    pass_on(3, 1)
     for q in range(3):
-        over_x(q).wait_recv()
-    cross_plane_ref[:, :, :, lanes(0)] = (
-        cross_half_ref[x, :, :, :, lanes(0)] + over_x_ref[0] + over_x_ref[1] + over_x_ref[2]
-    )
-    spread(lambda di, dj: cross_plane(0, di, dj))
-
-    def arrived_over(q, carry):
-        for s in range(1, 4):
-            over_y(q, s).wait_recv()
-            over_z(q, s).wait_recv()
-        return carry
-
-    lax.fori_loop(0, 4, arrived_over, 0)
-    cross_plane_ref[:, :, :, lanes(1)] = (
-        cross_half_ref[:, :, y, :, lanes(1)] + over_y_ref[0] + over_y_ref[1] + over_y_ref[2]
-    )
-    spread(lambda di, dj: cross_plane(1, di, dj))
-    cross_plane_ref[:, :, :, lanes(2)] = (
-        cross_half_ref[:, z, :, :, lanes(2)] + over_z_ref[0] + over_z_ref[1] + over_z_ref[2]
-    )
-    spread(lambda di, dj: cross_plane(2, di, dj))
-    pass_on(3)
-    for q in range(3):
-        total_side(q).wait_recv()
+        for half in range(2):
+            total_side(q, half).wait_recv()
     total_plane_ref[...] = total_half_ref[3] + total_side_ref[0] + total_side_ref[1] + total_side_ref[2]
 
     def total_plane(di, dj):
@@ -543,16 +523,18 @@
             total_plane_send,
             total_plane_recv,
             device(x=i, z=j),
-        ).start(0)
+        ).start()
 
     spread(total_plane)
-    for p in range(3):
-        axes = PARTS[p][3]
-        drain(cross_got_ref.at[pl.ds(1, 15), :, lanes(p)], cross_plane_recv.at[p])
-        acc = cross_plane_ref[at[axes[0]], at[axes[1]], :, lanes(p)]
+    for axis in "yxz":
+        axes = PLANE[axis]
+        drain(got_refs[axis].at[pl.ds(1, 15)], cross_plane_recv.at["xyz".index(axis)])
+        acc = plane_refs[axis][at[axes[0]], at[axes[1]]]
         for step in range(1, 16):
-            acc = acc + cross_got_ref[step, :, lanes(p)]
-        out_cross_ref[:, lanes(p)] = acc
+            acc = acc + got_refs[axis][step]
+        for name, q, begin, end, offset in PIECES:
+            if name == axis:
+                out_cross_ref[:, q * 256 + begin : q * 256 + end] = acc[:, offset : offset + end - begin]
     drain(total_got_ref.at[pl.ds(1, 15)], total_plane_recv)
     for half in range(2):
         acc = total_plane_ref[half, x, z]
@@ -563,22 +545,18 @@
 
     drain(message_ref.at[pl.ds(0, DEVICES - 1)], message_send)
 
-    def left(q, carry):
+    for q in range(4):
         cross_core(q).wait_send()
-        for s in range(1, 4):
-            over_y(q, s).wait_send()
-            over_z(q, s).wait_send()
-        return carry
-
-    lax.fori_loop(0, 4, left, 0)
-    for p in range(3):
-        over_x(p).wait_send()
-        drain(cross_got_ref.at[pl.ds(1, 15), :, lanes(p)], cross_plane_send.at[p])
+    for k in range(5):
+        for step in range(1, 4):
+            piece(k, step).wait_send()
+    for axis in "xyz":
+        drain(got_refs[axis].at[pl.ds(1, 15)], cross_plane_send.at["xyz".index(axis)])
     for q in range(4):
         for half in range(2):
             total_core(q, half).wait_send()
-        if q < 3:
-            total_side(q).wait_send()
+            if q < 3:
+                total_side(q, half).wait_send()
     drain(total_got_ref.at[pl.ds(1, 15)], total_plane_send)
 
 
@@ -625,14 +603,13 @@
             VMEM((1024, 128), F32),
             VMEM((FAR, D), BF),
             VMEM((M, 2 * DS, FAR), BF),
-            VMEM((4, 4, 2, 4, 8, D), F32),
+            VMEM((4, 4, 4, 2, 4, 8, 256), F32),
             VMEM((2, 4, 4, 2, 4, 8, 128), F32),
-            VMEM((4, 4, 4, 8, D), F32),
-            VMEM((3, 4, 4, 8, 384), F32),
-            VMEM((3, 4, 4, 8, 256), F32),
-            VMEM((3, 4, 4, 8, 384), F32),
-            VMEM((4, 4, 8, D), F32),
-            VMEM((16, 8, D), F32),
+            VMEM((4, 4, 4, 4, 8, 256), F32),
+            {axis: VMEM((3, 4, 4, 8, width), F32) for axis, width in WIDTH.items()},
+            VMEM((D, NEAR), BF),
+            {axis: VMEM((4, 4, 8, width), F32) for axis, width in WIDTH.items()},
+            {axis: VMEM((16, 8, width), F32) for axis, width in WIDTH.items()},
             VMEM((4, 2, 4, 4, 8, 128), F32),
             VMEM((3, 2, 4, 4, 8, 128), F32),
             VMEM((2, 4, 4, 8, 128), F32),
@@ -643,18 +620,14 @@
             DMA,
             DMA((4,)),
             DMA((4,)),
-            DMA((3,)),
-            DMA((3,)),
-            DMA((4, 3)),
-            DMA((4, 3)),
-            DMA((4, 3)),
-            DMA((4, 3)),
+            DMA((5, 3)),
+            DMA((5, 3)),
             DMA((3,)),
             DMA((3,)),
             DMA((4, 2)),
             DMA((4, 2)),
-            DMA((3,)),
-            DMA((3,)),
+            DMA((3, 2)),
+            DMA((3, 2)),
             DMA,
             DMA,
         ],

time: 65 us -> 63.1 us (0.971)
  Pallas kernels: 63.3 us -> 61.9 us
    pallas_call x1, Pallas kernels: 61.7 us -> 60.3 us  [per_device(): pl.pallas_call(kernel, out_shape=(jax.ShapeDtypeStruct((2, 8, 128), F32),...]
where the time goes in v6:
time: 63.1 us; the launch traced here: 62.5 us
  Pallas kernels  61.9 us (98%)
  between operations  0.64 us (1%)
    pallas_call x1, Pallas kernels, per_device(): pl.pallas_call(kernel, out_shape=(jax.ShapeDtypeStruct((2, 8, 128), F32),...  60.3 us
    pallas_call x1, Pallas kernels, per_device(): pl.pallas_call(finish_kernel, out_shape=(jax.ShapeDtypeStruct((16, 8, DS)...  1.58 us

profile of v6, /device:TPU:0, one launch (start us, length us, event | category | flops | bytes accessed | tf_op | source)
XLA Modules:
  0.0 62.5 jit_solution(9745742116138239916)
XLA Ops:
  0.6 60.3 %refine.1 = (f32[2,8,128]{2,1,0:T(8,128)}, f32[8,128]{1,0:T(8,128)}, f32[8,1024]{1,0:T(8,128)}) custom-call(s32[256]{0:T(256)} %coarse_smem.1, s32[1,256]{1,0:T(1,128)} %bitcast.9, s32[64,256]{1,0:T(8,128)} %bitcast.8, bf16[1024,256]{1,0:T(8,128)(2,1)} %bitcast.7, s32[4096,128]{1,0:T(8,128)} %bitcast.6, bf16[256,1024]{1,0:T(8,128)(2,1)} %vectors_hbm.1, ...), custom_call_target="tpu_custom_call" | custom-call | tf_op jit(solution)/shard_map/refine/pallas_call | solution.py:577
  60.9 1.6 %finish.1 = (f32[16,8,16]{2,1,0:T(8,128)}, f32[8,1024]{1,0:T(8,128)}) custom-call(f32[2,8,128]{2,1,0:T(8,128)} %get-tuple-element.5.total_ref, f32[8,128]{1,0:T(8,128)} %get-tuple-element.6.counts_ref, f32[8,1024]{1,0:T(8,128)} %get-tuple-element.7.cross_ref), custom_call_target="tpu_custom_call" | custom-call | tf_op jit(solution)/shard_map/finish/pallas_call | solution.py:648

commit v7 on v6

--- a/solution.py
+++ b/solution.py
@@ -152,16 +152,20 @@
             acc = acc + lax.dot_general(upper, lower, NT, preferred_element_type=F32)
         counts_ref[pl.ds(pl.multiple_of(lax.div(i, 2) * 32, 32), 32), :] += acc
 
-    def greet_and_count(i, carry):
+    def greet_rows(i, carry):
         for k in range(4):
             greet(i * 4 + k, 0)
-        count(i)
+        return carry
+
+    def count_step(i, carry):
+        count(i * 2)
+        count(i * 2 + 1)
         return carry
 
     for k in range(4):
         greet(k, 1 if k == 0 else 0)
-    count(jnp.int32(0))
-    lax.fori_loop(1, 8, greet_and_count, 0)
+    lax.fori_loop(1, 8, greet_rows, 0)
+    lax.fori_loop(0, 4, count_step, 0)
     for i in range(8):
         rows = pl.ds(i * 128, 128)
         table_book_ref[rows, :] = book_ref[rows, :].astype(F32)
@@ -286,23 +290,26 @@
     for i in range(8):
         near_xt_ref[i * 128 : (i + 1) * 128, :] = vectors_ref[:, i * 128 : (i + 1) * 128].T
 
-    def near_cross(q, carry):
-        rows = near_reb_ref[pl.ds(pl.multiple_of(q * 256, 256), 256), :]
-        for i in range(4):
-            block = lax.dot_general(near_xt_ref[i * 256 : (i + 1) * 256, :], rows, NT, preferred_element_type=F32)
-            cross_ref[q, i] = block.reshape(4, 2, 4, 8, 256)
-        return carry
-
-    lax.fori_loop(0, 4, near_cross, 0)
+    def near_cross(h, carry):
+        for k in range(2):
+            q = h * 2 + k
+            rows = near_reb_ref[pl.ds(pl.multiple_of(q * 256, 256), 256), :]
+            for i in range(4):
+                block = lax.dot_general(near_xt_ref[i * 256 : (i + 1) * 256, :], rows, NT, preferred_element_type=F32)
+                cross_ref[q, i] = block.reshape(4, 2, 4, 8, 256)
+        return carry
+
+    lax.fori_loop(0, 2, near_cross, 0)
     rotate(vectors_ref, NEAR, 0, 4)
 
-    def near_total(g, carry):
-        lower, upper = group(near_codes_ref, g, NEAR)
-        total_ref[g % 2, 0:2, :, :, g // 2] = lower.reshape(2, 4, 2, 8, 128)
-        total_ref[g % 2, 2:4, :, :, g // 2] = upper.reshape(2, 4, 2, 8, 128)
-        return carry
-
-    lax.fori_loop(0, 8, near_total, 0)
+    def near_total(i, carry):
+        for half in range(2):
+            lower, upper = group(near_codes_ref, i * 2 + half, NEAR)
+            total_ref[half, 0:2, :, :, i] = lower.reshape(2, 4, 2, 8, 128)
+            total_ref[half, 2:4, :, :, i] = upper.reshape(2, 4, 2, 8, 128)
+        return carry
+
+    lax.fori_loop(0, 4, near_total, 0)
 
     def widen(i, carry):
         chunk_load(i).wait()

time: 63.1 us -> 60.2 us (0.954)
  Pallas kernels: 61.9 us -> 59.2 us
    pallas_call x1, Pallas kernels: 60.3 us -> 57.6 us  [per_device(): pl.pallas_call(kernel, out_shape=(jax.ShapeDtypeStruct((2, 8, 128), F32),...]
where the time goes in v7:
time: 60.2 us; the launch traced here: 59.8 us
  Pallas kernels  59.2 us (98%)
  between operations  0.64 us (1%)
    pallas_call x1, Pallas kernels, per_device(): pl.pallas_call(kernel, out_shape=(jax.ShapeDtypeStruct((2, 8, 128), F32),...  57.6 us
    pallas_call x1, Pallas kernels, per_device(): pl.pallas_call(finish_kernel, out_shape=(jax.ShapeDtypeStruct((16, 8, DS)...  1.58 us

profile of v7, /device:TPU:0, one launch (start us, length us, event | category | flops | bytes accessed | tf_op | source)
XLA Modules:
  0.0 59.8 jit_solution(17700588234543181141)
XLA Ops:
  0.6 57.6 %refine.1 = (f32[2,8,128]{2,1,0:T(8,128)}, f32[8,128]{1,0:T(8,128)}, f32[8,1024]{1,0:T(8,128)}) custom-call(s32[256]{0:T(256)} %coarse_smem.1, s32[1,256]{1,0:T(1,128)} %bitcast.9, s32[64,256]{1,0:T(8,128)} %bitcast.8, bf16[1024,256]{1,0:T(8,128)(2,1)} %bitcast.7, s32[4096,128]{1,0:T(8,128)} %bitcast.6, bf16[256,1024]{1,0:T(8,128)(2,1)} %vectors_hbm.1, ...), custom_call_target="tpu_custom_call" | custom-call | tf_op jit(solution)/shard_map/refine/pallas_call | solution.py:584
  58.2 1.6 %finish.1 = (f32[16,8,16]{2,1,0:T(8,128)}, f32[8,1024]{1,0:T(8,128)}) custom-call(f32[2,8,128]{2,1,0:T(8,128)} %get-tuple-element.5.total_ref, f32[8,128]{1,0:T(8,128)} %get-tuple-element.6.counts_ref, f32[8,1024]{1,0:T(8,128)} %get-tuple-element.7.cross_ref), custom_call_target="tpu_custom_call" | custom-call | tf_op jit(solution)/shard_map/finish/pallas_call | solution.py:655

commit v8 on v7

--- a/solution.py
+++ b/solution.py
@@ -166,10 +166,6 @@
         greet(k, 1 if k == 0 else 0)
     lax.fori_loop(1, 8, greet_rows, 0)
     lax.fori_loop(0, 4, count_step, 0)
-    for i in range(8):
-        rows = pl.ds(i * 128, 128)
-        table_book_ref[rows, :] = book_ref[rows, :].astype(F32)
-
     slots_load.wait()
     for load in loads:
         load.start()
@@ -250,6 +246,10 @@
 
     for k in range(4):
         post(k, 1 if k == 0 else 0)
+    for i in range(8):
+        rows = pl.ds(i * 128, 128)
+        table_book_ref[rows, :] = book_ref[rows, :].astype(F32)
+
     lax.fori_loop(1, 8, post_and_decode, 0)
     near_decode(jnp.int32(0))
     arrived_ref[me] = message_ref[me]

time: 60.2 us -> 60.3 us (level)
  no operation moved by 1% of the time
where the time goes in v8:
time: 60.3 us; the launch traced here: 59.8 us
  Pallas kernels  59.2 us (98%)
  between operations  0.64 us (1%)
    pallas_call x1, Pallas kernels, per_device(): pl.pallas_call(kernel, out_shape=(jax.ShapeDtypeStruct((2, 8, 128), F32),...  57.6 us
    pallas_call x1, Pallas kernels, per_device(): pl.pallas_call(finish_kernel, out_shape=(jax.ShapeDtypeStruct((16, 8, DS)...  1.58 us

profile of v8, /device:TPU:0, one launch (start us, length us, event | category | flops | bytes accessed | tf_op | source)
XLA Modules:
  0.0 59.8 jit_solution(14893165865738886172)
XLA Ops:
  0.6 57.6 %refine.1 = (f32[2,8,128]{2,1,0:T(8,128)}, f32[8,128]{1,0:T(8,128)}, f32[8,1024]{1,0:T(8,128)}) custom-call(s32[256]{0:T(256)} %coarse_smem.1, s32[1,256]{1,0:T(1,128)} %bitcast.9, s32[64,256]{1,0:T(8,128)} %bitcast.8, bf16[1024,256]{1,0:T(8,128)(2,1)} %bitcast.7, s32[4096,128]{1,0:T(8,128)} %bitcast.6, bf16[256,1024]{1,0:T(8,128)(2,1)} %vectors_hbm.1, ...), custom_call_target="tpu_custom_call" | custom-call | tf_op jit(solution)/shard_map/refine/pallas_call | solution.py:584
  58.3 1.6 %finish.1 = (f32[16,8,16]{2,1,0:T(8,128)}, f32[8,1024]{1,0:T(8,128)}) custom-call(f32[2,8,128]{2,1,0:T(8,128)} %get-tuple-element.5.total_ref, f32[8,128]{1,0:T(8,128)} %get-tuple-element.6.counts_ref, f32[8,1024]{1,0:T(8,128)} %get-tuple-element.7.cross_ref), custom_call_target="tpu_custom_call" | custom-call | tf_op jit(solution)/shard_map/finish/pallas_call | solution.py:655
